TPU v7x, 128 devices: a whole 4x4x4 slice. The times are simulated.
128 devices in a mesh: grp: 8 (over x_lo, y), tile: 16 (over z, x_hi, core).
Axes of the slice: x: 4 (x_hi: 2, x_lo: 2; x = x_hi * 2 + x_lo), y: 4, z: 4, core: 2. Of those that a mesh axis runs over, the one named last changes fastest.
Arguments:
- field: bfloat16 [256, 128, 16, 128], P('tile', 'grp'), may hold values from -6 to 6
- sea: int32 [256, 128, 16], P('tile', 'grp'), may hold values 0 or 1
- conv_weight: bfloat16 [3, 3, 3, 128, 128], replicated, may hold values from -0.109375 to 0.109375
- lift_weight: bfloat16 [128, 1024], replicated, may hold values from -0.5 to 0.5
- mix_weight: bfloat16 [2, 1024, 1024], P(None, 'grp'), may hold values from -0.125 to 0.125
- proj_weight: bfloat16 [1024, 128], replicated, may hold values from -0.1875 to 0.1875
- kx_modes: int32 [32], replicated, may hold values from 0 to 127, as said below
- ky_modes: int32 [32], replicated, may hold values from 0 to 63, as said below
- kz_modes: int32 [4], replicated, may hold values from 0 to 7, as said below
- cotangent: bfloat16 [256, 128, 16, 128], P('tile', 'grp'), may hold values from -0.03125 to 0.03125
Outputs:
- output_cells: bfloat16 [256, 128, 16, 128], P('tile', 'grp')
- grad_conv: float32 [3, 3, 3, 128, 128], replicated
- grad_lift: float32 [128, 1024], replicated
- grad_mix: float32 [2, 1024, 1024], P(None, 'grp')
- grad_proj: float32 [1024, 128], replicated
Inputs may be any that keep to these rules, and one draw needn't show every extreme that they name: `kx_modes`: 32 distinct frequencies, 0 and 127 among them. `ky_modes`: 32 distinct frequencies, 0 and 63 among them. `kz_modes`: 4 distinct frequencies, 0 and 7 among them.
All inputs are finite; a program needn't handle non-finite values. No bound on the sum of `sea` on one device may be relied on, other than what follows from the above.
Results may differ from a plain program's by a relative error of at most 0.03.
Values may be sent and summed in bfloat16 or wider, within the bound.
A program may use at most 128 MiB of HBM per device.

v0:
```python
import math

import jax
import jax.numpy as jnp
from jax import lax
from jax.sharding import PartitionSpec as P

BX = 128
BY = 64
BZ = 8
KX = 32
KY = 32
KZ = 4


def extended(cells, sides, width):
    for axis, dim in sides:
        count = lax.axis_size(axis)
        ends = count - 1
        head = lax.slice_in_dim(cells, 0, width, axis=dim)
        tail = lax.slice_in_dim(cells, cells.shape[dim] - width, cells.shape[dim], axis=dim)
        cells = jnp.concatenate(
            [
                lax.ppermute(tail, axis, [(i, (i + 1) % count) for i in range(ends)]),
                cells,
                lax.ppermute(head, axis, [((i + 1) % count, i) for i in range(ends)]),
            ],
            axis=dim,
        )
    return cells


def phase_angles(freq_list, length):
    positions = jnp.arange(length, dtype=jnp.int32)
    turn_count = freq_list[:, None] * positions[None, :] % length
    return turn_count.astype(jnp.float32) * (2.0 * math.pi / length)


def make_plane(ky_modes, kz_modes):
    angles = (
        phase_angles(ky_modes, BY)[:, None, :, None] + phase_angles(kz_modes, BZ)[None, :, None, :]
    )
    result_table = jnp.stack([jnp.cos(angles), -jnp.sin(angles)], 0)
    return result_table.reshape(2 * KY * KZ, BY * BZ).astype(jnp.bfloat16)


def make_line(kx_modes):
    angles = phase_angles(kx_modes, BX)
    cosine = jnp.cos(angles)
    sine_vals = jnp.sin(angles)
    upper_rows = jnp.stack([cosine, sine_vals], 1)
    lower_rows = jnp.stack([-sine_vals, cosine], 1)
    return jnp.stack([upper_rows, lower_rows], 0).astype(jnp.bfloat16)


def stencil_offsets(padded):
    wide_y = padded.shape[1]
    wide_z = padded.shape[2]
    reach = wide_y * wide_z + wide_z + 1
    offsets = []
    for shift_x in range(3):
        for shift_y in range(3):
            for shift_z in range(3):
                offsets.append(
                    (
                        shift_x,
                        shift_y,
                        shift_z,
                        (shift_x - 1) * wide_y * wide_z + (shift_y - 1) * wide_z + (shift_z - 1),
                    )
                )
    return (reach, offsets)


def conv_cells(padded, conv_weight):
    channels = padded.shape[-1]
    flat_rows = padded.reshape(-1, channels)
    reach, offsets = stencil_offsets(padded)
    span = flat_rows.shape[0] - 2 * reach
    summed = None
    for shift_x, shift_y, shift_z, offset in offsets:
        window = lax.slice_in_dim(flat_rows, reach + offset, reach + offset + span, axis=0)
        product = jnp.dot(
            window, conv_weight[shift_x, shift_y, shift_z], preferred_element_type=jnp.float32
        )
        summed = product if summed is None else summed + product
    full = jnp.pad(summed, ((reach, reach), (0, 0))).reshape(
        padded.shape[0], padded.shape[1], padded.shape[2], -1
    )
    return full[1:-1, 1:-1, 1:-1].reshape(-1, conv_weight.shape[-1])


def conv_grads(padded, grad_rows, extent):
    size_x, size_y, size_z = extent
    channels = padded.shape[-1]
    out_channels = grad_rows.shape[-1]
    flat_rows = padded.reshape(-1, channels)
    reach, offsets = stencil_offsets(padded)
    span = flat_rows.shape[0] - 2 * reach
    grad_grid = jnp.pad(
        grad_rows.reshape(size_x, size_y, size_z, out_channels), ((1, 1), (1, 1), (1, 1), (0, 0))
    )
    grad_flat = lax.slice_in_dim(grad_grid.reshape(-1, out_channels), reach, reach + span, axis=0)
    pieces = []
    for shift_x, shift_y, shift_z, offset in offsets:
        window = lax.slice_in_dim(flat_rows, reach + offset, reach + offset + span, axis=0)
        pieces.append(
            lax.dot_general(
                window, grad_flat, (((0,), (0,)), ((), ())), preferred_element_type=jnp.float32
            )
        )
    return jnp.stack(pieces).reshape(3, 3, 3, channels, out_channels)


def block_mean(values):
    rows_x, rows_y, rows_z, channels = values.shape
    return (
        values.astype(jnp.float32)
        .reshape(rows_x // 2, 2, rows_y // 2, 2, rows_z // 2, 2, channels)
        .mean(axis=(1, 3, 5))
    )


def block_sum(values):
    rows_x, rows_y, rows_z, channels = values.shape
    return values.reshape(rows_x // 2, 2, rows_y // 2, 2, rows_z // 2, 2, channels).sum(
        axis=(1, 3, 5)
    )


def spread_blocks(values):
    rows_x, rows_y, rows_z, channels = values.shape
    spread = jnp.broadcast_to(
        values[:, None, :, None, :, None, :], (rows_x, 2, rows_y, 2, rows_z, 2, channels)
    )
    return spread.reshape(2 * rows_x, 2 * rows_y, 2 * rows_z, channels)


def gelu_back(inputs, upstream):
    return jax.vjp(jax.nn.gelu, inputs)[1](upstream)[0]


def left_dot(first, second):
    return lax.dot_general(
        first, second, (((0,), (0,)), ((), ())), preferred_element_type=jnp.float32
    )


def right_dot(first, second):
    return lax.dot_general(
        first, second, (((1,), (1,)), ((), ())), preferred_element_type=jnp.float32
    )


def mixing_grid(mix_weight):
    real_w = mix_weight[0]
    imag_w = mix_weight[1]
    return jnp.stack([jnp.stack([real_w, -imag_w]), jnp.stack([imag_w, real_w])])


def spectral_in(cell_vals, plane_tab, line_tab):
    partial_sum = jnp.einsum(
        "kn,xnw->xkw", plane_tab, cell_vals, preferred_element_type=jnp.float32
    )
    partial_sum = partial_sum.astype(jnp.bfloat16).reshape(
        cell_vals.shape[0], 2, KY, KZ, cell_vals.shape[2]
    )
    received = lax.all_to_all(partial_sum, "tile", split_axis=2, concat_axis=0, tiled=True)
    flat_part = received.reshape(received.shape[0], 2, -1)
    mode_vals = jnp.einsum("qkpx,xpr->qkr", line_tab, flat_part, preferred_element_type=jnp.float32)
    return mode_vals.reshape(2, KX, received.shape[2], KZ, received.shape[4]).astype(jnp.bfloat16)


def spectral_out(mode_vals, plane_tab, line_tab):
    flat_modes = mode_vals.reshape(2, KX, -1)
    inverse = jnp.einsum("qkpx,qkr->xpr", line_tab, flat_modes, preferred_element_type=jnp.float32)
    inverse = inverse.astype(jnp.bfloat16).reshape(
        BX, 2, mode_vals.shape[2], KZ, mode_vals.shape[4]
    )
    received = lax.all_to_all(inverse, "tile", split_axis=0, concat_axis=2, tiled=True)
    flat_recv = received.reshape(received.shape[0], 2 * KY * KZ, received.shape[4])
    return jnp.einsum("kn,xkw->xnw", plane_tab, flat_recv, preferred_element_type=jnp.float32)


def shards(
    field,
    sea,
    conv_weight,
    lift_weight,
    mix_weight,
    proj_weight,
    kx_modes,
    ky_modes,
    kz_modes,
    cotangent,
):
    size_x, size_y, size_z, channels = field.shape
    coarse_x = size_x // 2
    coarse_y = size_y // 2
    coarse_z = size_z // 2
    wide_w = lift_weight.shape[1]
    block_w = mix_weight.shape[1]
    extent = (size_x, size_y, size_z)
    sea_cells = sea.astype(jnp.bfloat16)[..., None]
    masked = field * sea_cells
    rimmed = extended(masked, (("grp", 1), ("tile", 0)), 1)
    padded = jnp.pad(rimmed, ((0, 0), (0, 0), (1, 1), (0, 0)))
    hidden_pre = conv_cells(padded, conv_weight)
    hidden = jax.nn.gelu(hidden_pre).astype(jnp.bfloat16).reshape(size_x, size_y, size_z, channels)
    coarse = block_mean(hidden).astype(jnp.bfloat16)
    coarse_rows = coarse.reshape(-1, channels)
    lifted_local = jnp.dot(coarse_rows, lift_weight, preferred_element_type=jnp.float32).astype(
        jnp.bfloat16
    )
    lifted = lax.all_to_all(
        lifted_local.reshape(coarse_x, coarse_y, coarse_z, wide_w),
        "grp",
        split_axis=3,
        concat_axis=1,
        tiled=True,
    )
    lifted = lifted.reshape(coarse_x, BY * BZ, block_w)
    plane_tab = make_plane(ky_modes, kz_modes)
    line_tab = make_line(kx_modes)
    spec_scale = 1.0 / math.sqrt(BX * BY * BZ * KX * KY * KZ)
    mixer = mixing_grid(mix_weight)
    modes_in = spectral_in(lifted, plane_tab, line_tab)
    local_modes = modes_in.reshape(2, -1, block_w)
    mix_terms = jnp.einsum("pcio,cmi->pmo", mixer, local_modes, preferred_element_type=jnp.float32)
    mixed = lax.psum_scatter(mix_terms.astype(jnp.bfloat16), "grp", scatter_dimension=2, tiled=True)
    spectral = spectral_out(mixed.reshape(modes_in.shape), plane_tab, line_tab)
    bottle_pre = spec_scale * spectral + lifted.astype(jnp.float32)
    bottle = jax.nn.gelu(bottle_pre).astype(jnp.bfloat16).reshape(coarse_x, BY, BZ, block_w)
    bottle_cells = lax.all_to_all(bottle, "grp", split_axis=1, concat_axis=3, tiled=True)
    bottle_rows = bottle_cells.reshape(-1, wide_w)
    projected = jnp.dot(bottle_rows, proj_weight, preferred_element_type=jnp.float32)
    projected = projected.reshape(coarse_x, coarse_y, coarse_z, channels)
    output_cells = (
        (hidden.astype(jnp.float32) + spread_blocks(projected)) * sea_cells.astype(jnp.float32)
    ).astype(jnp.bfloat16)
    out_grad = cotangent.astype(jnp.float32) * sea_cells.astype(jnp.float32)
    proj_grad = block_sum(out_grad).astype(jnp.bfloat16).reshape(-1, channels)
    grad_proj = left_dot(bottle_rows, proj_grad)
    bottle_grad = right_dot(proj_grad, proj_weight).astype(jnp.bfloat16)
    bottle_grad = lax.all_to_all(
        bottle_grad.reshape(coarse_x, coarse_y, coarse_z, wide_w),
        "grp",
        split_axis=3,
        concat_axis=1,
        tiled=True,
    )
    bottle_pre_grad = gelu_back(
        bottle_pre, bottle_grad.reshape(bottle_pre.shape).astype(jnp.float32)
    )
    space_grad = (spec_scale * bottle_pre_grad).astype(jnp.bfloat16)
    mixed_local = spectral_in(space_grad, plane_tab, line_tab)
    mixed_grad = lax.all_gather(mixed_local, "grp", axis=4, tiled=True).reshape(2, -1, wide_w)
    swapped = jnp.stack([mixed_grad[1], -mixed_grad[0]])
    grad_mix = jnp.stack(
        [
            jnp.einsum("cmi,cmo->io", local_modes, mixed_grad, preferred_element_type=jnp.float32),
            jnp.einsum("cmi,cmo->io", local_modes, swapped, preferred_element_type=jnp.float32),
        ]
    )
    modes_grad = jnp.einsum(
        "pcio,pmo->cmi", mixer, mixed_grad, preferred_element_type=jnp.float32
    ).astype(jnp.bfloat16)
    lifted_spec = spectral_out(modes_grad.reshape(modes_in.shape), plane_tab, line_tab)
    lifted_grad = (bottle_pre_grad + lifted_spec).astype(jnp.bfloat16)
    lifted_back = lax.all_to_all(
        lifted_grad.reshape(coarse_x, BY, BZ, block_w),
        "grp",
        split_axis=1,
        concat_axis=3,
        tiled=True,
    )
    lifted_rows = lifted_back.reshape(-1, wide_w)
    coarse_grad = right_dot(lifted_rows, lift_weight)
    grad_lift = left_dot(coarse_rows, lifted_rows)
    hidden_grad = out_grad + 0.125 * spread_blocks(
        coarse_grad.reshape(coarse_x, coarse_y, coarse_z, channels)
    )
    hidden_pre_grad = gelu_back(hidden_pre, hidden_grad.reshape(-1, channels)).astype(jnp.bfloat16)
    grad_conv = conv_grads(padded, hidden_pre_grad, extent)
    grad_mix = lax.psum(grad_mix.astype(jnp.bfloat16), "tile").astype(jnp.float32)
    grad_conv, grad_proj, grad_lift = lax.psum((grad_conv, grad_proj, grad_lift), ("grp", "tile"))
    return (output_cells, grad_conv, grad_lift, grad_mix, grad_proj)


def solution(mesh):
    return jax.shard_map(
        shards,
        mesh=mesh,
        in_specs=(
            P("tile", "grp", None, None),
            P("tile", "grp", None),
            P(),
            P(),
            P(None, "grp", None),
            P(),
            P(),
            P(),
            P(),
            P("tile", "grp", None, None),
        ),
        out_specs=(P("tile", "grp", None, None), P(), P(), P(None, "grp", None), P()),
        check_vma=False,
    )
```

profile of v0, /device:TPU:1, one launch (start us, length us, event | category | flops | bytes accessed | tf_op | source)
XLA Modules:
  0.0 751.5 jit_solution(2394296603077343614)
XLA Ops:
  8.2 1.7 broadcast_multiply_fusion
  11.2 4.7 collective-permute-start
  17.2 3.8 collective-permute-start.3
  21.0 4.6 collective-permute-start.2
  27.1 2.8 select_maximum_fusion
  29.9 2.6 reshape.374
  46.8 1.8 pad.13
  48.6 4.4 reshape.375
  53.0 4.0 fusion.277
  57.0 3.0 reduce_sum.18
  60.5 22.6 %copy.181 = bf16[8,8,8,1024]{2,1,0,3:T(8,128)(2,1)} copy(bf16[8,8,8,1024]{3,2,1,0:T(8,128)(2,1)S(1)} %bitcast.431) | data formatting | bytes 2097152 | tf_op jit(solution)/shard_map/reshape | solution.py:216
  83.1 20.5 %reshape.425 = bf16[8,2,32768]{2,1,0:T(2,128)(2,1)} reshape(bf16[1024,8,8,8]{3,2,1,0:T(8,128)(2,1)} %bitcast.416) | data formatting | bytes 2097152
  103.5 7.9 %all-to-all-start = ((bf16[8,2,32768]{2,1,0:T(2,128)(2,1)}), bf16[8,2,32768]{2,1,0:T(2,128)(2,1)S(1)}, u32[]{:S(2)}, u32[]{:S(2)}) async-start(bf16[8,2,32768]{2,1,0:T(2,128)(2,1)} %reshape.425), calls=%async_computation | async-start | bytes 2097152 | tf_op jit(solution)/shard_map/all_to_all | solution.py:215
  111.6 2.0 add_cosine_fusion
  113.8 3.1 copy.184
  116.9 7.1 reshape.402
  125.2 20.7 %reshape.426 = bf16[1024,8,8,8]{3,2,1,0:T(8,128)(2,1)} reshape(bf16[8,2,32768]{2,1,0:T(2,128)(2,1)S(1)} %all-to-all-done) | data formatting | bytes 2097152
  145.9 14.5 %copy.183 = bf16[8,8,8,8,128]{4,3,2,1,0:T(8,128)(2,1)S(1)} copy(bf16[8,8,8,8,128]{3,2,0,4,1:T(8,128)(2,1)} %bitcast.417) | data formatting | bytes 2097152 | tf_op jit(solution)/shard_map/all_to_all | solution.py:215
  161.7 2.1 copy.186
  163.8 1.9 copy.187
  165.7 9.6 %all-to-all-start.1 = ((bf16[8,2,32,4,128]{4,0,3,1,2:T(8,128)(2,1)}), bf16[8,2,32,4,128]{4,0,3,1,2:T(8,128)(2,1)}, u32[]{:S(2)}, u32[]{:S(2)}) async-start(bf16[8,2,32,4,128]{4,0,3,1,2:T(8,128)(2,1)} %copy.187), calls=%async_computation.1 | async-start | bytes 1048576 | tf_op jit(solution)/shard_map/all_to_all | solution.py:168
  177.5 9.2 %all-to-all-done.1 = bf16[8,2,32,4,128]{4,0,3,1,2:T(8,128)(2,1)} async-done(((bf16[8,2,32,4,128]{4,0,3,1,2:T(8,128)(2,1)}), bf16[8,2,32,4,128]{4,0,3,1,2:T(8,128)(2,1)}, u32[]{:S(2)}, u32[]{:S(2)}) %all-to-all-start.1) | async-done | bytes 524320 | tf_op jit(solution)/shard_map/all_to_all | solution.py:168
  186.7 2.1 copy.296
  188.9 2.2 reshape.380
  191.0 2.0 copy.189
  194.5 2.7 fusion.20
  197.2 3.8 copy.245
  201.0 2.4 copy.247
  203.4 3.2 convert_multiply_fusion
  206.6 3.0 reduce_sum.19
  211.0 23.1 %copy.203 = bf16[8,8,8,1024]{2,1,0,3:T(8,128)(2,1)} copy(bf16[8,8,8,1024]{3,2,1,0:T(8,128)(2,1)} %bitcast.432) | data formatting | bytes 2097152 | tf_op jit(solution)/shard_map/reshape | solution.py:246
  234.1 20.5 %reshape.427 = bf16[8,2,32768]{2,1,0:T(2,128)(2,1)} reshape(bf16[1024,8,8,8]{3,2,1,0:T(8,128)(2,1)} %bitcast.418) | data formatting | bytes 2097152
  254.6 4.2 all-to-all-start.4
  262.7 2.2 copy.193
  264.9 8.2 %all-to-all-done.4 = bf16[8,2,32768]{2,1,0:T(2,128)(2,1)} async-done(((bf16[8,2,32768]{2,1,0:T(2,128)(2,1)}), bf16[8,2,32768]{2,1,0:T(2,128)(2,1)}, u32[]{:S(2)}, u32[]{:S(2)}) %all-to-all-start.4) | async-done | bytes 1048608 | tf_op jit(solution)/shard_map/all_to_all | solution.py:245
  273.1 5.5 all-to-all-start.2
  278.6 21.6 %reshape.428 = bf16[1024,8,8,8]{3,2,1,0:T(8,128)(2,1)} reshape(bf16[8,2,32768]{2,1,0:T(2,128)(2,1)} %all-to-all-done.4) | data formatting | bytes 2097152
  300.2 16.8 %copy.204 = bf16[8,8,8,1024]{3,2,1,0:T(8,128)(2,1)} copy(bf16[8,8,8,1024]{2,1,0,3:T(8,128)(2,1)} %bitcast.419) | data formatting | bytes 2097152 | tf_op jit(solution)/shard_map/all_to_all | solution.py:245
  318.5 1.6 copy.205
  320.2 2.9 copy.206
  326.1 4.1 fusion.13
  332.4 18.4 %all_to_all.114 = bf16[8,2,32,4,128]{4,0,3,1,2:T(8,128)(2,1)S(1)} all-to-all(bf16[8,2,32,4,128]{4,0,3,1,2:T(8,128)(2,1)S(1)} %copy.209), channel_id=1, replica_groups=mesh['grp'=8,'tile'=16] {'tile'}, dimensions={2} | all-to-all | bytes 1048576 | tf_op jit(solution)/shard_map/all_to_all | solution.py:168
  352.7 1.6 copy.198
  355.6 3.6 all-to-all-start.3
  359.2 30.6 %all-gather.2.cloned.1.call-done = bf16[2,32,2,4,1024]{4,1,3,2,0:T(8,128)(2,1)} async-done(((bf16[2,32,2,4,128]{4,1,3,2,0:T(8,128)(2,1)}), bf16[2,32,2,4,1024]{4,1,3,2,0:T(8,128)(2,1)}) %all-gather.2.cloned.1.call-update) | async-done | bytes 1048592 | tf_op jit(solution)/shard_map/all_gather | solution.py:257
  389.8 2.4 copy.213
  393.4 2.0 fusion.22
  395.5 2.2 copy.217
  397.7 13.1 %all-to-all-start.6 = ((bf16[128,2,2,4,128]{4,3,2,1,0:T(4,128)(2,1)}), bf16[128,2,2,4,128]{4,3,2,1,0:T(4,128)(2,1)}, u32[]{:S(2)}, u32[]{:S(2)}) async-start(bf16[128,2,2,4,128]{4,3,2,1,0:T(4,128)(2,1)} %copy.217), calls=%async_computation.6 | async-start | bytes 1048576 | tf_op jit(solution)/shard_map/all_to_all | solution.py:180
  412.3 2.2 copy.200
  414.5 7.6 %all-to-all-done.6 = bf16[128,2,2,4,128]{4,3,2,1,0:T(4,128)(2,1)} async-done(((bf16[128,2,2,4,128]{4,3,2,1,0:T(4,128)(2,1)}), bf16[128,2,2,4,128]{4,3,2,1,0:T(4,128)(2,1)}, u32[]{:S(2)}, u32[]{:S(2)}) %all-to-all-start.6) | async-done | bytes 524320 | tf_op jit(solution)/shard_map/all_to_all | solution.py:180
  428.1 4.4 all-to-all-start.7
  432.6 2.5 fusion.278
  442.5 4.6 all-to-all-done.7
  447.1 2.0 convolution_multiply_fusion
  451.6 3.0 fusion.7
  454.6 1.9 pad.14
  456.5 3.8 reshape.396
  460.4 2.0 fusion.118
  487.2 2.5 copy.223
  493.1 86.4 %all-reduce.7.cloned.1.call-done = bf16[2,128,1024]{2,1,0:T(8,128)(2,1)} async-done(((bf16[2,128,1024]{2,1,0:T(8,128)(2,1)}), bf16[2,128,1024]{2,1,0:T(8,128)(2,1)}) %all-reduce.7.cloned.1.call-update) | async-done | bytes 524304 | tf_op jit(solution)/shard_map/psum | solution.py:285
  579.5 2.1 convert_element_type.230
  581.7 158.3 %all-reduce.9.cloned.1.call-done = (f32[3,3,3,128,128]{4,3,2,1,0:T(8,128)}, f32[128,1024]{1,0:T(8,128)}, f32[1024,128]{1,0:T(8,128)}) async-done(((f32[3,3,3,128,128]{4,3,2,1,0:T(8,128)}, f32[128,1024]{1,0:T(8,128)}, f32[1024,128]{1,0:T(8,128)}), (f32[3,3,3,128,128]{4,3,2,1,0:T(8,128)}, f32[128,1024]{1,0:T(8,128)}, f32[1024,128]{1,0:T(8,128)})) %all-reduce.9.cloned.1.call-update) | async-done | bytes 2818064 | tf_op jit(solution)/shard_map/psum | solution.py:286
  740.0 3.0 copy.327
  (180 shorter events, 89.3 us)
Async XLA Ops:
  7.2 202.4 %copy-start = (bf16[1024,128]{1,0:T(8,128)(2,1)S(1)}, bf16[1024,128]{1,0:T(8,128)(2,1)}, u32[]{:S(2)}) copy-start(bf16[1024,128]{1,0:T(8,128)(2,1)} %param.15) | copy-start | bytes 786436
  9.9 6.0 collective-permute-start.1
  11.2 6.0 collective-permute-start
  17.2 8.5 %collective-permute-start.3 = (bf16[1,18,16,128]{3,2,1,0:T(8,128)(2,1)S(1)}, bf16[1,18,16,128]{3,2,1,0:T(8,128)(2,1)S(1)}, u32[]{:S(2)}, u32[]{:S(2)}) collective-permute-start(bf16[1,18,16,128]{3,2,1,0:T(8,128)(2,1)S(1)} %get-tuple-element.15), channel_id=1, source_target_pairs={{1,0},{2,1},{3,2},{4,3},{5,4},{6,5},{7,6},{8,7},{9,8},{10,9},{11,1... | collective-permute-start | bytes 221192 | tf_op jit(solution)/shard_map/ppermute | solution.py:26
  21.0 6.0 collective-permute-start.2
  29.9 2.6 copy-start.15
  57.0 3.1 copy-start.20
  60.1 23.0 %copy-start.12 = (bf16[8,8,8,128]{3,2,1,0:T(8,128)(2,1)}, bf16[8,8,8,128]{3,2,1,0:T(8,128)(2,1)S(1)}, u32[]{:S(2)}) copy-start(bf16[8,8,8,128]{3,2,1,0:T(8,128)(2,1)S(1)} %copy.180) | copy-start | bytes 393220
  103.5 7.9 %copy-start.24 = (s32[4]{0:T(128)S(1)}, s32[4]{0:T(128)}, u32[]{:S(2)}) copy-start(s32[4]{0:T(128)} %param.18) | copy-start | bytes 52
  103.5 8.0 %copy-start.25 = (s32[32]{0:T(128)S(1)}, s32[32]{0:T(128)}, u32[]{:S(2)}) copy-start(s32[32]{0:T(128)} %param.17) | copy-start | bytes 388
  103.5 21.6 %all-to-all-start = ((bf16[8,2,32768]{2,1,0:T(2,128)(2,1)}), bf16[8,2,32768]{2,1,0:T(2,128)(2,1)S(1)}, u32[]{:S(2)}, u32[]{:S(2)}) async-start(bf16[8,2,32768]{2,1,0:T(2,128)(2,1)} %reshape.425), calls=%async_computation | async-start | bytes 2097152 | tf_op jit(solution)/shard_map/all_to_all | solution.py:215
  116.9 7.1 copy-start.26
  165.7 21.0 %all-to-all-start.1 = ((bf16[8,2,32,4,128]{4,0,3,1,2:T(8,128)(2,1)}), bf16[8,2,32,4,128]{4,0,3,1,2:T(8,128)(2,1)}, u32[]{:S(2)}, u32[]{:S(2)}) async-start(bf16[8,2,32,4,128]{4,0,3,1,2:T(8,128)(2,1)} %copy.187), calls=%async_computation.1 | async-start | bytes 1048576 | tf_op jit(solution)/shard_map/all_to_all | solution.py:168
  175.3 83.6 %reduce-scatter.4.cloned.1.call-start = ((), (), s32[]{:S(2)}) async-start(), calls=%async_computation.11 | async-start | bytes 1179648
  194.4 6.6 copy-start.10
  194.5 6.5 copy-start.22
  254.6 18.5 %all-to-all-start.4 = ((bf16[8,2,32768]{2,1,0:T(2,128)(2,1)}), bf16[8,2,32768]{2,1,0:T(2,128)(2,1)}, u32[]{:S(2)}, u32[]{:S(2)}) async-start(bf16[8,2,32768]{2,1,0:T(2,128)(2,1)} %reshape.427), calls=%async_computation.4 | async-start | bytes 2097152 | tf_op jit(solution)/shard_map/all_to_all | solution.py:245
  273.1 51.3 %all-to-all-start.2 = ((bf16[128,2,2,4,128]{4,3,2,1,0:T(4,128)(2,1)}), bf16[128,2,2,4,128]{4,3,2,1,0:T(4,128)(2,1)}, u32[]{:S(2)}, u32[]{:S(2)}) async-start(bf16[128,2,2,4,128]{4,3,2,1,0:T(4,128)(2,1)} %copy.193), calls=%async_computation.2 | async-start | bytes 1048576 | tf_op jit(solution)/shard_map/all_to_all | solution.py:180
  278.6 111.2 %all-gather.2.cloned.1.call-start = ((), (), s32[]{:S(2)}) async-start(), calls=%async_computation.9 | async-start | bytes 1179648 | tf_op jit(solution)/shard_map/all_gather | solution.py:257
  324.4 1.7 copy-start.7
  330.2 1.3 copy-start.4
  355.6 42.1 %all-to-all-start.3 = ((bf16[8,64,8,128]{3,2,0,1:T(8,128)(2,1)}), bf16[8,64,8,128]{3,2,0,1:T(8,128)(2,1)S(1)}, u32[]{:S(2)}, u32[]{:S(2)}) async-start(bf16[8,64,8,128]{3,2,0,1:T(8,128)(2,1)} %copy.199), calls=%async_computation.3 | async-start | bytes 2097152 | tf_op jit(solution)/shard_map/all_to_all | solution.py:234
  389.8 2.4 copy-start.16
  389.8 2.4 copy-start.17
  397.7 24.4 %all-to-all-start.6 = ((bf16[128,2,2,4,128]{4,3,2,1,0:T(4,128)(2,1)}), bf16[128,2,2,4,128]{4,3,2,1,0:T(4,128)(2,1)}, u32[]{:S(2)}, u32[]{:S(2)}) async-start(bf16[128,2,2,4,128]{4,3,2,1,0:T(4,128)(2,1)} %copy.217), calls=%async_computation.6 | async-start | bytes 1048576 | tf_op jit(solution)/shard_map/all_to_all | solution.py:180
  422.1 1.7 copy-start.5
  428.1 6.9 copy-start.3
  428.1 19.0 %all-to-all-start.7 = ((bf16[8,64,8,128]{3,2,0,1:T(8,128)(2,1)}), bf16[8,64,8,128]{3,2,0,1:T(8,128)(2,1)}, u32[]{:S(2)}, u32[]{:S(2)}) async-start(bf16[8,64,8,128]{3,2,0,1:T(8,128)(2,1)} %copy.222), calls=%async_computation.7 | async-start | bytes 2097152 | tf_op jit(solution)/shard_map/all_to_all | solution.py:270
  432.5 147.0 %all-reduce.7.cloned.1.call-start = ((), (), s32[]{:S(2)}) async-start(), calls=%async_computation.10 | async-start | bytes 1048576 | tf_op jit(solution)/shard_map/psum | solution.py:285
  436.3 3.3 copy-start.23
  437.3 4.0 copy-start.11
  441.2 5.9 copy-start.21
  442.5 297.5 %all-reduce.9.cloned.1.call-start = ((), (), s32[]{:S(2)}) async-start(), calls=%async_computation.12 | async-start | bytes 5636096 | tf_op jit(solution)/shard_map/psum | solution.py:286
  447.1 2.8 copy-start.14
  449.1 1.5 copy-start.6
  449.2 2.4 copy-start.2
  460.3 2.0 copy-start.9
  487.2 2.5 copy-start.13
  491.9 1.2 copy-start.8
  740.0 3.0 copy-start.19
  740.0 3.8 copy-start.18
  740.0 4.6 copy-start.1
Sparse Core Ops, SparseCore 0:
  203.5 31.3 reduce-scatter.3
  352.8 36.9 all-gather.1
  442.6 136.9 all-reduce.6
  586.2 153.7 all-reduce.8
where the time goes:
time: 764 us; the launch traced here: 751 us
  waiting for transfers between devices  309 us (40%)
  local copies, waits for them, and re-layouts  247 us (32%)
  matrix products  67.6 us (9%)
  starting transfers between devices  62.8 us (8%)
  other arithmetic  31.6 us (4%)
  blocking collectives  18.4 us (2%)
  between operations  15.2 us (2%)
    psum x1, waiting for transfers between devices, shards(): lax.psum((grad_conv, grad_proj, grad_lift), ('grp', 'tile'))  158 us
    unnamed x65, local copies, waits for them, and re-layouts  99.9 us
    psum x1, waiting for transfers between devices, shards(): lax.psum(grad_mix.astype(jnp.bfloat16), 'tile').astype(jnp.float32)  86.4 us
    all_gather x1, waiting for transfers between devices, shards(): lax.all_gather(mixed_local, 'grp', axis=4, tiled=True)  30.6 us
    dot_general x27, matrix products, conv_grads(): lax.dot_general(window, grad_flat, (((0,), (0,)), ((), ())), preferred_el...  27.7 us
    reshape x1, local copies, waits for them, and re-layouts, shards(): bottle_grad.reshape(coarse_x, coarse_y, coarse_z, wide_w)  23.1 us
    reshape x1, local copies, waits for them, and re-layouts, shards(): lifted_local.reshape(coarse_x, coarse_y, coarse_z, wide_w)  22.6 us
    all_to_all x2, starting transfers between devices, spectral_out(): lax.all_to_all(inverse, 'tile', split_axis=0, concat_axis=2, tiled=True)  18.6 us
  transfers between devices with their start and end apart: 15, of which 11 were waited for; matrix products, arithmetic and copies ran while one was open for 25% of the time, Pallas kernels for 0%

commit v1 on v0

v1 whole, which is shorter than its diff:
```python
import math

import jax
import jax.numpy as jnp
from jax import lax
from jax.experimental import pallas as pl
from jax.experimental.pallas import tpu as pltpu
from jax.sharding import PartitionSpec as P

BX = 128
BY = 64
BZ = 8
KX = 32
KY = 32
KZ = 4
C = 128
W = 1024
GRP = 8
TILE = 16
PAIRS = 8
SCALE = 1.0 / math.sqrt(BX * BY * BZ * KX * KY * KZ)
ROOT = math.sqrt(2.0 / math.pi)
CUBE = 0.044715
F32 = jnp.float32
BF16 = jnp.bfloat16
MESH = pl.DeviceIdType.MESH


def dot(first, second, left=1, right=0):
    return lax.dot_general(
        first, second, (((left,), (right,)), ((), ())), preferred_element_type=F32
    )


def grid_of(shape, dim):
    return lax.broadcasted_iota(jnp.int32, shape, dim)


def cos_sin(turns, length):
    angles = (turns & (length - 1)).astype(F32) * (2.0 * math.pi / length)
    return jnp.cos(angles), jnp.sin(angles)


def z_table(kz):
    shape = (64, 128)
    row, lane = grid_of(shape, 0), grid_of(shape, 1)
    freq = jnp.concatenate([jnp.full((16, 128), kz[b], jnp.int32) for b in range(KZ)], 0)
    cosine, sine = cos_sin(freq * (lane & 7), BZ)
    p, s = (row >> 3) & 1, lane >> 6
    value = jnp.where(s == p, jnp.where(s == 0, cosine, -cosine), -sine)
    return jnp.where((row & 7) == ((lane >> 3) & 7), value, 0.0)


def y_table(ky, first):
    shape = (32, 128)
    row, lane = grid_of(shape, 0), grid_of(shape, 1)
    freq = jnp.zeros(shape, jnp.int32)
    for a in range(16):
        freq = jnp.where((row >> 1) == a, ky[first + a], freq)
    y = ((lane >> 4) << 3) + (lane & 7)
    cosine, sine = cos_sin(freq * y, BY)
    p, q = (lane >> 3) & 1, row & 1
    return jnp.where(p == q, cosine, jnp.where(q == 0, sine, -sine))


def x_table(kx):
    shape = (32, 256)
    row, lane = grid_of(shape, 0), grid_of(shape, 1)
    freq = jnp.zeros(shape, jnp.int32)
    for k in range(KX):
        freq = jnp.where(row == k, kx[k], freq)
    x = ((lane >> 4) << 3) + (lane & 7)
    cosine, sine = cos_sin(freq * x, BX)
    even = ((lane >> 3) & 1) == 0
    return jnp.concatenate(
        [jnp.where(even, cosine, sine), jnp.where(even, -sine, cosine)], 0
    )


def spot(axis):
    return lax.axis_index(axis)


def place():
    grp, tile = spot("grp"), spot("tile")
    return {
        "xlo": grp // 4,
        "y": lax.rem(grp, 4),
        "z": tile // 4,
        "xhi": lax.rem(tile // 2, 2),
        "core": lax.rem(tile, 2),
    }


LENGTHS = {"xlo": 2, "y": 4, "z": 4, "xhi": 2, "core": 2}
DIGITS = {"ring_y": ("y",), "ring_z": ("z",), "xz": ("xlo", "z", "xhi"), "xy": ("xlo", "y", "xhi")}


def digits_of(name, number):
    digits = {}
    for part in reversed(DIGITS[name]):
        digits[part] = number % LENGTHS[part]
        number //= LENGTHS[part]
    return digits


def own(name):
    if name not in DIGITS:
        return spot(name)
    here = place()
    index = 0
    for part in DIGITS[name]:
        index = index * LENGTHS[part] + here[part]
    return index


def group(name):
    if name not in DIGITS:
        count = GRP if name == "grp" else TILE
        for away in range(1, count):
            index = lax.rem(spot(name) + away, count)
            yield away, index, {name: index}
        return
    count = math.prod(LENGTHS[part] for part in DIGITS[name])
    for away in range(1, count):
        there = place()
        index = 0
        for part, step in digits_of(name, away).items():
            if step:
                there[part] = lax.rem(there[part] + step, LENGTHS[part])
        for part in DIGITS[name]:
            index = index * LENGTHS[part] + there[part]
        device = {
            "grp": there["xlo"] * 4 + there["y"],
            "tile": there["z"] * 4 + there["xhi"] * 2 + there["core"],
        }
        yield away, index, device


def partner():
    tile = spot("tile")
    return {"tile": tile + 1 - 2 * lax.rem(tile, 2)}


def near(step_tile, step_grp):
    target = {}
    if step_tile:
        target["tile"] = lax.rem(spot("tile") + step_tile + TILE, TILE)
    if step_grp:
        target["grp"] = lax.rem(spot("grp") + step_grp + GRP, GRP)
    return target


DIAGONALS = ((1, 1), (1, -1), (-1, 1), (-1, -1))


def greet():
    barrier = pltpu.get_barrier_semaphore()
    targets = [device for name in ("grp", "tile") for _, _, device in group(name)]
    targets += [near(*step) for step in DIAGONALS]
    for away, _, device in group("xz"):
        steps = digits_of("xz", away)
        if steps["xlo"] and (steps["z"] or steps["xhi"]):
            targets.append(device)
    for away, _, device in group("xy"):
        steps = digits_of("xy", away)
        if steps["xhi"] and steps["y"]:
            targets.append(device)
    for device in targets:
        pl.semaphore_signal(barrier, inc=1, device_id=device, device_id_type=MESH)
    return lambda: pl.semaphore_wait(barrier, len(targets))


def remote(src, dst, sems, place, device):
    copy = pltpu.make_async_remote_copy(
        src_ref=src,
        dst_ref=dst,
        send_sem=sems.at[0, place],
        recv_sem=sems.at[1, place],
        device_id=device,
        device_id_type=MESH,
    )
    copy.start()
    return copy


def scatter_rows(src, slots, sems, name):
    return [
        remote(src.at[index], slots.at[away], sems, away, device)
        for away, index, device in group(name)
    ]


def add_rows(src, slots, copies, name):
    total = src[own(name)].astype(F32)
    for place, copy in enumerate(copies):
        copy.wait_recv()
        total += slots[place + 1].astype(F32)
    return total.astype(BF16)


def exchange(src, dst, sems, name):
    me = own(name)
    copies = [
        remote(src.at[index], dst.at[me], sems, away, device) for away, index, device in group(name)
    ]
    dst[me] = src[me]
    return copies


def spread_rows(src, dst, sems, name):
    me = own(name)
    copies = [remote(src, dst.at[me], sems, away, device) for away, index, device in group(name)]
    dst[me] = src[...]
    return copies


def arrived(copies):
    for copy in copies:
        copy.wait_recv()


def left(copies):
    for copy in copies:
        copy.wait_send()


def pair_sems(count):
    return pltpu.SemaphoreType.DMA((2, count))


def held(*shape, dtype=BF16):
    return pltpu.VMEM(shape, dtype)


FILTER_SCRATCH = (
    lambda: [held(KZ, 8, 16, C)]
    + [held(GRP, 8, 16, C) for _ in range(3)]
    + [held(TILE, 16, C) for _ in range(4)]
    + [held(256, C, dtype=F32)]
    + [pair_sems(GRP), pair_sems(TILE), pair_sems(TILE), pair_sems(GRP)]
)


def x_filter(y_tab, x_tab, work, beside):
    part, got_y, sent, back, mid, got, turned, home, wide, sem1, sem2, sem3, sem4 = work
    me = spot("grp")
    first = [
        remote(part.at[index // 2], got_y.at[me], sem1, away, device)
        for away, index, device in group("grp")
    ]
    got_y[me] = part[me // 2]
    beside[0]()
    arrived(first)
    for x in range(8):
        rows = got_y[:, x].reshape(128, C)
        wide[pl.ds(x, 32, stride=8), :] = dot(y_tab[...], rows)
    mid[...] = wide[...].astype(BF16).reshape(mid.shape)
    second = exchange(mid, got, sem2, "tile")
    beside[1]()
    arrived(second)
    modes = dot(x_tab[...], got[...].reshape(TILE * 16, C)).astype(BF16)
    turned[...] = dot(x_tab[...], modes, 0, 0).astype(BF16).reshape(turned.shape)
    third = exchange(turned, home, sem3, "tile")
    beside[2]()
    arrived(third)
    wide[...] = home[...].reshape(256, C).astype(F32)
    for x in range(8):
        rows = wide[pl.ds(x, 32, stride=8), :].astype(BF16)
        sent[:, x] = dot(y_tab[...], rows, 0, 0).astype(BF16).reshape(GRP, 16, C)
    fourth = exchange(sent, back, sem4, "grp")
    beside[3]()
    arrived(fourth)
    for copies in (first, second, third, fourth):
        left(copies)


SUM_SCRATCH = (
    lambda: [held(2, 4, 16, 16, C) for _ in range(2)]
    + [held(4, 16, 16, C) for _ in range(2)]
    + [held(16, 16, C) for _ in range(4)]
    + [held(16, C) for _ in range(2)]
    + [held(16, 16, C) for _ in range(2)]
    + [pair_sems(16) for _ in range(10)]
)


class Sums:
    def __init__(self, x, y, work):
        self.x, self.y = x, y
        self.buffers, self.sems = work[:12], work[12:]
        self.sent = []

    def run(self, step):
        x, y, s = self.x, self.y, self.sems
        got, mine, sa, sb, ma, mb, ra, rb, ta, tb, ga, gb = self.buffers
        core = place()["core"]
        if step == 0:
            self.a = [remote(x.at[1 - core], got, s[0], 0, partner())]
            self.b = []
        if step == 1:
            arrived(self.a)
            mine[...] = (x[core].astype(F32) + got[...].astype(F32)).astype(BF16)
            self.a = scatter_rows(mine.at[0], sa, s[1], "ring_y")
            self.b = scatter_rows(mine.at[1], sb, s[2], "ring_z")
        if step == 2:
            ma[...] = add_rows(mine.at[0], sa, self.a, "ring_y")
            self.a = scatter_rows(ma, ra, s[3], "xz")
            mb[...] = add_rows(mine.at[1], sb, self.b, "ring_z")
            self.b = scatter_rows(mb, rb, s[4], "xy")
        if step == 3:
            ta[...] = add_rows(ma, ra, self.a, "xz")
            self.a = spread_rows(ta, ga, s[5], "xz")
            tb[...] = add_rows(mb, rb, self.b, "xy")
            self.b = spread_rows(tb, gb, s[6], "xy")
        if step == 4:
            arrived(self.a)
            self.a = spread_rows(ga, y.at[core, 0], s[7], "ring_y")
            arrived(self.b)
            self.b = spread_rows(gb, y.at[core, 1], s[8], "ring_z")
        if step == 5:
            arrived(self.a)
            arrived(self.b)
            self.a = [remote(y.at[core], y.at[core], s[9], 0, partner())]
            self.b = []
        if step == 6:
            arrived(self.a)
            for copies in self.sent:
                left(copies)
            return
        self.sent += [self.a, self.b]


def block_at(n):
    return n // 16, n // 8 % 2, n % 8 // 2, pl.ds(8 * (n % 2), 8)


def tanh_of(x):
    return jnp.tanh(ROOT * (x + CUBE * x * x * x))


def gelu_slope(x, t):
    return 0.5 * (1.0 + t) + 0.5 * x * (1.0 - t * t) * (ROOT * (1.0 + 3.0 * CUBE * x * x))


def shift_rows(rows, forward):
    z = lax.rem(lax.broadcasted_iota(jnp.int32, rows.shape, 0), 16)
    if forward:
        return jnp.where(z == 0, 0.0, pltpu.roll(rows, 1, 0))
    return jnp.where(z == 15, 0.0, pltpu.roll(rows, rows.shape[0] - 1, 0))


def pool(rows, tmp):
    tmp[...] = rows.reshape(8, 2, 16, C).sum(1).reshape(128, C)
    return tmp[pl.ds(0, 64, stride=2), :] + tmp[pl.ds(1, 64, stride=2), :]


def unpool(rows, tmp):
    tmp[pl.ds(0, 64, stride=2), :] = rows
    tmp[pl.ds(1, 64, stride=2), :] = rows
    wide = jnp.broadcast_to(tmp[...].reshape(8, 1, 16, C), (8, 2, 16, C))
    return wide.reshape(256, C)


def step_kernel(
    field_in,
    sea_in,
    cot_in,
    conv_in,
    lift_in,
    mix_in,
    proj_in,
    kx,
    ky,
    kz,
    out,
    sums,
    taps,
    lift_parts,
    field,
    sea,
    cot,
    conv_w,
    lift,
    mix,
    proj,
    load_sems,
    x_tab,
    y_tab,
    z_tab,
    z_cells,
    z_twice,
    rim,
    rim_t,
    halo_x,
    halo_y,
    halo_c,
    conv_flat,
    pre,
    hidden,
    feats,
    proj_grad,
    lift_own,
    lm_part,
    lm_slots,
    lm_mine,
    lm_all,
    stacked,
    bottle_pre,
    bottle_grad,
    bottle,
    bpg,
    direct,
    cell_grad,
    acc,
    sums_in,
    taps_in,
    lift_mine,
    tmp,
    sem_halo,
    sem_lm1,
    sem_lm2,
    sem_lm3,
    sem_lift,
    *work,
):
    count = len(FILTER_SCRATCH())
    filter1, filter2 = work[:count], work[count : 2 * count]
    work = work[2 * count :]
    count = len(SUM_SCRATCH())
    first_sums = Sums(sums_in, sums, work[:count])
    last_sums = Sums(taps_in, taps, work[count:])
    grp, tile = spot("grp"), spot("tile")
    core = place()["core"]
    loads = []
    for i, (src, dst) in enumerate(
        (
            (field_in, field),
            (sea_in, sea),
            (conv_in, conv_w),
            (lift_in, lift),
            (mix_in, mix),
            (cot_in, cot),
            (proj_in, proj),
        )
    ):
        loads.append(pltpu.make_async_copy(src, dst, load_sems.at[i]))
        loads[i].start()
    met = greet()
    for copy in loads[:2]:
        copy.wait()

    @pl.loop(0, 16)
    def _(x):
        rim[x + 1, 1:17] = field[x] * sea[x]

    met()

    inner = pl.ds(1, 16)
    halos = [
        remote(rim.at[16, inner], halo_x.at[0], sem_halo, 0, near(1, 0)),
        remote(rim.at[1, inner], halo_x.at[1], sem_halo, 1, near(-1, 0)),
        remote(rim.at[inner, 16], halo_y.at[0], sem_halo, 2, near(0, 1)),
        remote(rim.at[inner, 1], halo_y.at[1], sem_halo, 3, near(0, -1)),
        remote(rim.at[16, 16], halo_c.at[0], sem_halo, 4, near(1, 1)),
        remote(rim.at[16, 1], halo_c.at[1], sem_halo, 5, near(1, -1)),
        remote(rim.at[1, 16], halo_c.at[2], sem_halo, 6, near(-1, 1)),
        remote(rim.at[1, 1], halo_c.at[3], sem_halo, 7, near(-1, -1)),
    ]
    for copy in loads[2:]:
        copy.wait()
    lift_own[...] = lift[:, pl.ds(pl.multiple_of(grp * C, C), C)]
    product = dot(lift_own[...], mix[core]).astype(BF16)
    for j in range(GRP):
        lm_part[j] = product[:, C * j : C * (j + 1)]

    for a in range(3):
        for b in range(3):
            for c in range(3):
                conv_flat[pl.ds(C * (3 * a + b), C), pl.ds(C * c, C)] = conv_w[a, b, c]

    @pl.loop(0, 8)
    def _(i):
        total = cot[2 * i].astype(F32) * sea[2 * i].astype(F32)
        total += cot[2 * i + 1].astype(F32) * sea[2 * i + 1].astype(F32)
        rows = pool(total.reshape(256, C), tmp)
        proj_grad[pl.ds(pl.multiple_of(64 * i, 64), 64), :] = rows.astype(BF16)

    stacked[pl.ds(0, C), :] = lift[...]
    x_tab[...] = x_table(kx).astype(BF16)
    y_tab[...] = y_table(ky, 16 * lax.rem(grp, 2)).astype(BF16)
    z_values = z_table(kz).astype(BF16)
    z_tab[...] = z_values
    z_cells[...] = z_values[:, :64]
    for j in range(GRP):
        z_twice[pl.ds(16 * j, 16), :] = z_values[16 * (j // 2) : 16 * (j // 2 + 1)]

    arrived(halos)
    lm_first = scatter_rows(lm_part, lm_slots, sem_lm1, "grp")
    sides = (tile > 0, tile < TILE - 1, grp > 0, grp < GRP - 1)

    def keep(flag, rows):
        return jnp.where(flag, rows, jnp.zeros_like(rows))

    for side, x in ((0, 0), (1, 17)):
        rim[x, 1:17] = keep(sides[side], halo_x[side])
    for side, y in ((0, 0), (1, 17)):
        rim[1:17, y] = keep(sides[2 + side], halo_y[side])
    for i, x, y in ((0, 0, 0), (1, 0, 17), (2, 17, 0), (3, 17, 17)):
        flag = jnp.logical_and(sides[0 if x == 0 else 1], sides[2 if y == 0 else 3])
        rim[x, y] = keep(flag, halo_c[i])

    def convolve(x):
        window = jnp.concatenate(
            [rim[x + a, b : b + 16].reshape(256, C) for a in range(3) for b in range(3)], 1
        )
        product = dot(window, conv_flat[...])
        rows = (
            product[:, C : 2 * C]
            + shift_rows(product[:, :C], True)
            + shift_rows(product[:, 2 * C :], False)
        )
        pre[x] = rows
        hidden[x] = (0.5 * rows * (1.0 + tanh_of(rows))).astype(BF16)

    pl.loop(0, 16)(convolve)

    for i in range(8):
        total = hidden[2 * i].astype(F32) + hidden[2 * i + 1].astype(F32)
        coarse = (0.125 * pool(total, tmp)).astype(BF16)
        feats[pl.ds(64 * i, 64), pl.ds(0, C)] = coarse
        filter1[0][:, i] = dot(z_cells[...], coarse).astype(BF16).reshape(KZ, 16, C)

    def turn_windows():
        @pl.loop(0, 18)
        def _(x):
            for b in range(3):
                rim_t[x, pl.ds(C * b, C), :] = rim[x, b : b + 16].reshape(256, C).T

    def back_through():
        for j in range(4):
            cols = pl.ds(256 * j, 256)
            bottle_grad[:, cols] = dot(proj_grad[...], proj[cols, :], 1, 1).astype(BF16)

    lm = {}

    def gather_lm():
        lm_mine[...] = add_rows(lm_part, lm_slots, lm_first, "grp")
        lm["grp"] = spread_rows(lm_mine, lm_all.at[core], sem_lm2, "grp")
        back_through()

    def swap_lm():
        arrived(lm["grp"])
        lm["core"] = [remote(lm_all.at[core], lm_all.at[core], sem_lm3, 0, partner())]

    x_filter(y_tab, x_tab, filter1, (turn_windows, gather_lm, lambda: None, swap_lm))

    arrived(lm["core"])
    for p in range(2):
        for j in range(GRP):
            stacked[pl.ds(C * (p + 1), C), pl.ds(C * j, C)] = lm_all[p, j]
    for copies in (lm_first, lm["grp"], lm["core"]):
        left(copies)

    for i in range(8):
        modes = filter1[3][:, i].reshape(128, C)
        both = (SCALE * dot(z_twice[...], modes, 0, 0)).astype(BF16)
        feats[pl.ds(64 * i, 64), pl.ds(C, C)] = both[:64]
        feats[pl.ds(64 * i, 64), pl.ds(2 * C, C)] = both[64:]

    for j in range(4):
        cols = pl.ds(256 * j, 256)
        bottle_pre[...] = dot(feats[...], stacked[:, cols])

        @pl.loop(0, 8)
        def _(r):
            rows = pl.ds(pl.multiple_of(64 * r, 64), 64)
            v = bottle_pre[rows, :]
            t = tanh_of(v)
            bottle[rows, cols] = (0.5 * v * (1.0 + t)).astype(BF16)
            bpg[rows, cols] = (bottle_grad[rows, cols].astype(F32) * gelu_slope(v, t)).astype(BF16)

    feats_grad = dot(bpg[...], stacked[...], 1, 1)
    direct[...] = feats_grad[:, :C]
    pair_grad = (SCALE * feats_grad[:, C:]).astype(BF16)
    for i in range(8):
        rows = pair_grad[64 * i : 64 * (i + 1)]
        stacked_rows = jnp.concatenate([rows[:, :C], rows[:, C:]], 0)
        filter2[0][:, i] = dot(z_tab[...], stacked_rows).astype(BF16).reshape(KZ, 16, C)

    def weight_sums():
        for j in range(GRP):
            cols = pl.ds(C * j, C)
            outer = dot(feats[...], bpg[:, cols], 0, 0).astype(BF16)
            for k in range(3):
                rows = outer[C * k : C * (k + 1)]
                sums_in[block_at(8 * k + j)] = rows.reshape(8, 16, C)
            rows = dot(bottle[:, cols], proj_grad[...], 0, 0).astype(BF16)
            sums_in[block_at(24 + j)] = rows.reshape(8, 16, C)
        first_sums.run(0)

    def write_cells():
        direct_out = dot(bottle[...], proj[...])
        for i in range(8):
            cell_grad[i] = direct_out[64 * i : 64 * (i + 1)]

        @pl.loop(0, 8)
        def _(i):
            spread = unpool(cell_grad[i], tmp)
            for half in range(2):
                x = 2 * i + half
                value = (hidden[x].astype(F32) + spread).reshape(16, 16, C)
                out[x] = (value * sea[x].astype(F32)).astype(BF16)

    x_filter(
        y_tab,
        x_tab,
        filter2,
        (weight_sums, lambda: first_sums.run(1), write_cells, lambda: first_sums.run(2)),
    )

    for i in range(8):
        modes = filter2[3][:, i].reshape(128, C)
        rows = dot(z_twice[...], modes, 0, 0)[:64] + direct[pl.ds(64 * i, 64), :]
        cell_grad[i] = 0.125 * rows
    acc[...] = jnp.zeros_like(acc)

    def tap_grads(i):
        spread = unpool(cell_grad[i], tmp)
        total = None
        for half in range(2):
            x = 2 * i + half
            upstream = (cot[x].astype(F32) * sea[x].astype(F32)).reshape(256, C) + spread
            value = pre[x]
            grad = (upstream * gelu_slope(value, tanh_of(value))).astype(BF16).astype(F32)
            shifted = jnp.concatenate(
                [shift_rows(grad, False), grad, shift_rows(grad, True)], 1
            ).astype(BF16)
            windows = rim_t[pl.ds(x, 3)].reshape(9 * C, 256)
            product = dot(windows, shifted)
            total = product if total is None else total + product
        acc[...] += total

    pl.loop(0, 4)(tap_grads)
    first_sums.run(3)
    pl.loop(4, 8)(tap_grads)

    for c in range(3):
        for ab in range(9):
            n = 9 * c + ab
            rows = acc[pl.ds(C * ab, C), pl.ds(C * c, C)].astype(BF16)
            taps_in[block_at(n)] = rows.reshape(8, 16, C)
    for n in range(27, 32):
        taps_in[block_at(n)] = jnp.zeros((8, 16, C), BF16)
    last_sums.run(0)
    first_sums.run(4)
    last_sums.run(1)
    first_sums.run(5)
    last_sums.run(2)
    first_sums.run(6)
    last_sums.run(3)

    total = jnp.zeros((C, C), F32)
    for p in range(2):
        for j in range(GRP):
            cols = pl.ds(C * j, C)
            grads = sums[block_at(8 * (1 + p) + j)].reshape(C, C)
            total += dot(grads, mix[p, :, cols], 1, 1)
    lift_mine[...] = total.astype(BF16)
    lift_copies = spread_rows(lift_mine, lift_parts, sem_lift, "grp")
    last_sums.run(4)
    arrived(lift_copies)
    left(lift_copies)
    last_sums.run(5)
    last_sums.run(6)
    left(halos)


def finish_kernel(out_in, sums, taps, lift_parts, lift_own, out, conv, lift, mix, proj, sem):
    copy = pltpu.make_async_copy(out_in, out, sem)
    copy.start()
    for c in range(3):
        for ab in range(9):
            conv[3 * ab + c] = taps[9 * c + ab].astype(F32)
    for j in range(GRP):
        cols = pl.ds(C * j, C)
        lift[:, cols] = sums[j].astype(F32) + lift_parts[j].astype(F32)
        proj[j] = sums[24 + j].astype(F32)
        for p in range(2):
            mix[p, :, cols] = dot(lift_own[...], sums[8 * (1 + p) + j], 0, 0)
    copy.wait()


def shards(
    field,
    sea,
    conv_weight,
    lift_weight,
    mix_weight,
    proj_weight,
    kx_modes,
    ky_modes,
    kz_modes,
    cotangent,
):
    sea_cells = jnp.broadcast_to(sea.astype(BF16)[..., None], field.shape)
    vmem = pl.BlockSpec(memory_space=pltpu.VMEM)
    smem = pl.BlockSpec(memory_space=pltpu.SMEM)
    hbm = pl.BlockSpec(memory_space=pl.ANY)
    out, sums, taps, lift_parts = pl.pallas_call(
        step_kernel,
        out_shape=(
            jax.ShapeDtypeStruct(field.shape, BF16),
            jax.ShapeDtypeStruct((2, 2, 4, 16, 16, C), BF16),
            jax.ShapeDtypeStruct((2, 2, 4, 16, 16, C), BF16),
            jax.ShapeDtypeStruct((GRP, C, C), BF16),
        ),
        in_specs=[hbm] * 7 + [smem] * 3,
        out_specs=(vmem,) * 4,
        scratch_shapes=[
            held(16, 16, 16, C),
            held(16, 16, 16, C),
            held(16, 16, 16, C),
            held(3, 3, 3, C, C),
            held(C, W),
            held(2, C, W),
            held(W, C),
            pltpu.SemaphoreType.DMA((7,)),
            held(64, 256),
            held(32, 128),
            held(64, 128),
            held(64, 64),
            held(128, 128),
            held(18, 18, 16, C),
            held(18, 3 * C, 256),
            held(2, 16, 16, C),
            held(2, 16, 16, C),
            held(4, 16, C),
            held(9 * C, 3 * C),
            held(16, 256, C, dtype=F32),
            held(16, 256, C),
            held(512, 3 * C),
            held(512, C),
            held(C, C),
            held(GRP, C, C),
            held(GRP, C, C),
            held(C, C),
            held(2, GRP, C, C),
            held(3 * C, W),
            held(512, 256, dtype=F32),
            held(512, W),
            held(512, W),
            held(512, W),
            held(512, C, dtype=F32),
            held(8, 64, C, dtype=F32),
            held(9 * C, 3 * C, dtype=F32),
            held(2, 2, 4, 16, 16, C),
            held(2, 2, 4, 16, 16, C),
            held(C, C),
            held(128, C, dtype=F32),
            pair_sems(8),
            pair_sems(GRP),
            pair_sems(GRP),
            pair_sems(1),
            pair_sems(GRP),
        ]
        + FILTER_SCRATCH()
        + FILTER_SCRATCH()
        + SUM_SCRATCH()
        + SUM_SCRATCH(),
        compiler_params=pltpu.CompilerParams(
            collective_id=1, has_side_effects=True, vmem_limit_bytes=56 * 2**20
        ),
        name="step",
    )(
        field,
        sea_cells,
        cotangent,
        conv_weight,
        lift_weight,
        mix_weight,
        proj_weight,
        kx_modes,
        ky_modes,
        kz_modes,
    )
    lift_own = lax.dynamic_slice_in_dim(lift_weight, lax.axis_index("grp") * C, C, 1)
    out, conv, lift, mix, proj = pl.pallas_call(
        finish_kernel,
        out_shape=(
            jax.ShapeDtypeStruct(field.shape, BF16),
            jax.ShapeDtypeStruct((27, C, C), F32),
            jax.ShapeDtypeStruct((C, W), F32),
            jax.ShapeDtypeStruct((2, C, W), F32),
            jax.ShapeDtypeStruct((GRP, C, C), F32),
        ),
        in_specs=[hbm] + [vmem] * 4,
        out_specs=(hbm,) + (vmem,) * 4,
        scratch_shapes=[pltpu.SemaphoreType.DMA(())],
        compiler_params=pltpu.CompilerParams(vmem_limit_bytes=32 * 2**20),
        name="finish",
    )(out, sums.reshape(32, C, C), taps.reshape(32, C, C), lift_parts, lift_own)
    return (out, conv.reshape(3, 3, 3, C, C), lift, mix, proj.reshape(W, C))


def solution(mesh):
    return jax.shard_map(
        shards,
        mesh=mesh,
        in_specs=(
            P("tile", "grp", None, None),
            P("tile", "grp", None),
            P(),
            P(),
            P(None, "grp", None),
            P(),
            P(),
            P(),
            P(),
            P("tile", "grp", None, None),
        ),
        out_specs=(P("tile", "grp", None, None), P(), P(), P(None, "grp", None), P()),
        check_vma=False,
    )
```

time: 764 us -> 128 us (0.17); the launches traced: 751 us -> 127 us
  waiting for transfers between devices: 309 us -> 0 us
  local copies, waits for them, and re-layouts: 247 us -> 6.96 us
  Pallas kernels: 0 us -> 119 us
  matrix products: 67.6 us -> 0 us
  starting transfers between devices: 62.8 us -> 0 us
  other arithmetic: 31.6 us -> 0.91 us
  blocking collectives: 18.4 us -> 0 us
  between operations: 15.2 us -> 0.82 us
    psum x2 -> x0, waiting for transfers between devices: 245 us -> none  [the longest x1 158 us: shards(): lax.psum((grad_conv, grad_proj, grad_lift), ('grp', 'tile'))]
    pallas_call x0 -> x2, Pallas kernels: none -> 119 us  [the longest x1 116 us: shards(): pl.pallas_call(step_kernel, out_shape=(jax.ShapeDtypeStruct(field.shape,...]
    unnamed x65 -> x8, local copies, waits for them, and re-layouts: 99.9 us -> 4.62 us
    reshape x14 -> x0, local copies, waits for them, and re-layouts: 69.3 us -> none  [the longest x1 23.1 us: shards(): bottle_grad.reshape(coarse_x, coarse_y, coarse_z, wide_w)]
    dot_general x72 -> x0, matrix products: 67.6 us -> none  [the longest x27 27.7 us: conv_grads(): lax.dot_general(window, grad_flat, (((0,), (0,)), ((), ())), preferred_el...]
    all_to_all x7 -> x0, starting transfers between devices: 48.2 us -> none  [the longest x2 18.6 us: spectral_out(): lax.all_to_all(inverse, 'tile', split_axis=0, concat_axis=2, tiled=True)]
    all_to_all x10 -> x0, local copies, waits for them, and re-layouts: 41.4 us -> none  [the longest x1 16.8 us: shards(): lax.all_to_all(bottle_grad.reshape(coarse_x, coarse_y, coarse_z, wide_w),...]
    all_to_all x7 -> x0, waiting for transfers between devices: 30.7 us -> none  [the longest x1 9.19 us: spectral_in(): lax.all_to_all(partial_sum, 'tile', split_axis=2, concat_axis=0, tiled=True)]
  transfers between devices with their start and end apart: 15 -> 0, of which waited for: 11 -> 0; matrix products, arithmetic and copies ran while one was open for 25% -> 0% of each run, Pallas kernels for 0% -> 0%
where the time goes in v1:
time: 128 us; the launch traced here: 127 us
  Pallas kernels  119 us (93%)
  local copies, waits for them, and re-layouts  6.96 us (5%)
    pallas_call x1, Pallas kernels, shards(): pl.pallas_call(step_kernel, out_shape=(jax.ShapeDtypeStruct(field.shape,...  116 us
    unnamed x8, local copies, waits for them, and re-layouts  4.62 us
    pallas_call x1, Pallas kernels, shards(): pl.pallas_call(finish_kernel, out_shape=(jax.ShapeDtypeStruct(field.shape...  3.11 us

profile of v1, /device:TPU:1, one launch (start us, length us, event | category | flops | bytes accessed | tf_op | source)
XLA Modules:
  0.0 127.4 jit_solution(15637377326930646097)
XLA Ops:
  0.6 0.8 constant_dynamic-slice_fusion.lift_own
  1.4 0.9 convert_element_type.3
  2.3 1.6 %broadcast_in_dim.2.sea_in = bf16[16,16,16,128]{3,2,1,0:T(8,128)(2,1)} broadcast(bf16[16,16,16]{2,1,0:T(8,128)(2,1)S(1)} %convert_element_type.3), dimensions={0,1,2} | broadcast | bytes 1056768 | tf_op jit(solution)/shard_map/broadcast_in_dim | solution.py:706
  3.9 115.6 %step.1 = (bf16[16,16,16,128]{3,2,1,0:T(8,128)(2,1)}, bf16[2,2,4,16,16,128]{5,4,3,2,1,0:T(8,128)(2,1)}, bf16[2,2,4,16,16,128]{5,4,3,2,1,0:T(8,128)(2,1)}, bf16[8,128,128]{2,1,0:T(8,128)(2,1)}) custom-call(bf16[16,16,16,128]{3,2,1,0:T(8,128)(2,1)} %field_in.1, bf16[16,16,16,128]{3,2,1,0:T(8,128)(2,1)} %broadcast_in_dim.2.sea_in, ...), custom_call_target="tpu_custom_call" | custom-call | tf_op jit(solution)/shard_map/step/pallas_call | solution.py:710
  119.5 0.0 copy-start
  119.5 1.2 copy-done
  120.7 0.0 copy-start.1
  120.7 1.2 copy-done.1
  121.9 0.0 copy-start.2
  121.9 1.2 copy-done.2
  123.1 0.0 copy-start.3
  123.1 0.9 copy-done.3
  124.1 3.1 %finish.1 = (bf16[16,16,16,128]{3,2,1,0:T(8,128)(2,1)}, f32[27,128,128]{2,1,0:T(8,128)}, f32[128,1024]{1,0:T(8,128)}, f32[2,128,1024]{2,1,0:T(8,128)}, f32[8,128,128]{2,1,0:T(8,128)}) custom-call(bf16[16,16,16,128]{3,2,1,0:T(8,128)(2,1)S(1)} %copy-done, bf16[32,128,128]{2,1,0:T(8,128)(2,1)S(1)} %bitcast.4, bf16[32,128,128]{2,1,0:T(8,128)(2,1)S(1)} %bitcast.5, ...), custom_call_target="tpu_custom_call" | custom-call | tf_op jit(solution)/shard_map/finish/pallas_call | solution.py:788
Async XLA Ops:
  119.5 1.2 copy-start
  120.7 1.2 copy-start.1
  121.9 1.2 copy-start.2
  123.1 0.9 copy-start.3

commit v2 on v1

--- a/solution.py
+++ b/solution.py
@@ -93,7 +93,15 @@
 
 
 LENGTHS = {"xlo": 2, "y": 4, "z": 4, "xhi": 2, "core": 2}
-DIGITS = {"ring_y": ("y",), "ring_z": ("z",), "xz": ("xlo", "z", "xhi"), "xy": ("xlo", "y", "xhi")}
+DIGITS = {
+    "grp": ("xlo", "y"),
+    "tile": ("z", "xhi", "core"),
+    "ring_y": ("y",),
+    "ring_z": ("z",),
+    "xz": ("xlo", "z", "xhi"),
+    "xy": ("xlo", "y", "xhi"),
+}
+HOPS = {"xlo": (0, 1), "y": (0, 1, 2, 1), "z": (0, 1, 2, 1), "xhi": (0, 2), "core": (0, 0)}
 
 
 def digits_of(name, number):
@@ -104,9 +112,11 @@
     return digits
 
 
+def size_of(name):
+    return math.prod(LENGTHS[part] for part in DIGITS[name])
+
+
 def own(name):
-    if name not in DIGITS:
-        return spot(name)
     here = place()
     index = 0
     for part in DIGITS[name]:
@@ -115,14 +125,10 @@
 
 
 def group(name):
-    if name not in DIGITS:
-        count = GRP if name == "grp" else TILE
-        for away in range(1, count):
-            index = lax.rem(spot(name) + away, count)
-            yield away, index, {name: index}
-        return
-    count = math.prod(LENGTHS[part] for part in DIGITS[name])
-    for away in range(1, count):
+    def hops(away):
+        return sum(HOPS[part][step] for part, step in digits_of(name, away).items())
+
+    for away in sorted(range(1, size_of(name)), key=lambda away: (-hops(away), away)):
         there = place()
         index = 0
         for part, step in digits_of(name, away).items():
@@ -186,16 +192,16 @@
 
 def scatter_rows(src, slots, sems, name):
     return [
-        remote(src.at[index], slots.at[away], sems, away, device)
+        (away, remote(src.at[index], slots.at[away], sems, away, device))
         for away, index, device in group(name)
     ]
 
 
 def add_rows(src, slots, copies, name):
     total = src[own(name)].astype(F32)
-    for place, copy in enumerate(copies):
+    for away, copy in reversed(copies):
         copy.wait_recv()
-        total += slots[place + 1].astype(F32)
+        total += slots[away].astype(F32)
     return total.astype(BF16)
 
 
@@ -222,6 +228,7 @@
 
 def left(copies):
     for copy in copies:
+        copy = copy[1] if isinstance(copy, tuple) else copy
         copy.wait_send()
 
 
@@ -286,8 +293,8 @@
 
 
 class Sums:
-    def __init__(self, x, y, work):
-        self.x, self.y = x, y
+    def __init__(self, x, y, last, work):
+        self.x, self.y, self.last = x, y, last
         self.buffers, self.sems = work[:12], work[12:]
         self.sent = []
 
@@ -321,7 +328,7 @@
         if step == 5:
             arrived(self.a)
             arrived(self.b)
-            self.a = [remote(y.at[core], y.at[core], s[9], 0, partner())]
+            self.a = [remote(y.at[core], self.last.at[core], s[9], 0, partner())]
             self.b = []
         if step == 6:
             arrived(self.a)
@@ -373,11 +380,12 @@
     kx,
     ky,
     kz,
-    out,
-    sums,
-    taps,
-    lift_parts,
+    out_to,
+    sums_to,
+    taps_to,
+    lift_to,
     field,
+    sea_wide,
     sea,
     cot,
     conv_w,
@@ -391,12 +399,13 @@
     z_cells,
     z_twice,
     rim,
-    rim_t,
+    upstream,
     halo_x,
     halo_y,
     halo_c,
     conv_flat,
     pre,
+    base,
     hidden,
     feats,
     proj_grad,
@@ -417,6 +426,11 @@
     taps_in,
     lift_mine,
     tmp,
+    out,
+    sums,
+    taps,
+    lift_parts,
+    store_sems,
     sem_halo,
     sem_lm1,
     sem_lm2,
@@ -428,15 +442,19 @@
     filter1, filter2 = work[:count], work[count : 2 * count]
     work = work[2 * count :]
     count = len(SUM_SCRATCH())
-    first_sums = Sums(sums_in, sums, work[:count])
-    last_sums = Sums(taps_in, taps, work[count:])
+    first_sums = Sums(sums_in, sums, sums, work[:count])
+    last_sums = Sums(taps_in, taps, taps_to, work[count:])
     grp, tile = spot("grp"), spot("tile")
     core = place()["core"]
+
+    def sea_of(x):
+        return sea[pl.ds(pl.multiple_of(256 * x, 256), 256), :].reshape(16, 16, C)
+
     loads = []
     for i, (src, dst) in enumerate(
         (
             (field_in, field),
-            (sea_in, sea),
+            (sea_in, sea_wide),
             (conv_in, conv_w),
             (lift_in, lift),
             (mix_in, mix),
@@ -446,13 +464,30 @@
     ):
         loads.append(pltpu.make_async_copy(src, dst, load_sems.at[i]))
         loads[i].start()
+    stores = [
+        pltpu.make_async_copy(src, dst, store_sems.at[i])
+        for i, (src, dst) in enumerate(
+            ((out, out_to), (sums, sums_to), (lift_parts, lift_to), (taps.at[core], taps_to.at[core]))
+        )
+    ]
     met = greet()
-    for copy in loads[:2]:
-        copy.wait()
+    x_tab[...] = x_table(kx).astype(BF16)
+    y_tab[...] = y_table(ky, 16 * lax.rem(grp, 2)).astype(BF16)
+    z_values = z_table(kz).astype(BF16)
+    z_tab[...] = z_values
+    z_cells[...] = z_values[:, :64]
+    for j in range(GRP):
+        z_twice[pl.ds(16 * j, 16), :] = z_values[16 * (j // 2) : 16 * (j // 2 + 1)]
+    loads[1].wait()
+    lines = sea_wide[...].reshape(256, 16).astype(F32).astype(BF16)
+    for z in range(16):
+        pick = (grid_of((16, C), 0) == z).astype(F32).astype(BF16)
+        sea[pl.ds(z, 256, stride=16), :] = dot(lines, pick)
+    loads[0].wait()
 
     @pl.loop(0, 16)
     def _(x):
-        rim[x + 1, 1:17] = field[x] * sea[x]
+        rim[x + 1, 1:17] = (field[x].astype(F32) * sea_of(x)).astype(BF16)
 
     met()
 
@@ -481,20 +516,12 @@
 
     @pl.loop(0, 8)
     def _(i):
-        total = cot[2 * i].astype(F32) * sea[2 * i].astype(F32)
-        total += cot[2 * i + 1].astype(F32) * sea[2 * i + 1].astype(F32)
+        total = cot[2 * i].astype(F32) * sea_of(2 * i)
+        total += cot[2 * i + 1].astype(F32) * sea_of(2 * i + 1)
         rows = pool(total.reshape(256, C), tmp)
         proj_grad[pl.ds(pl.multiple_of(64 * i, 64), 64), :] = rows.astype(BF16)
 
     stacked[pl.ds(0, C), :] = lift[...]
-    x_tab[...] = x_table(kx).astype(BF16)
-    y_tab[...] = y_table(ky, 16 * lax.rem(grp, 2)).astype(BF16)
-    z_values = z_table(kz).astype(BF16)
-    z_tab[...] = z_values
-    z_cells[...] = z_values[:, :64]
-    for j in range(GRP):
-        z_twice[pl.ds(16 * j, 16), :] = z_values[16 * (j // 2) : 16 * (j // 2 + 1)]
-
     arrived(halos)
     lm_first = scatter_rows(lm_part, lm_slots, sem_lm1, "grp")
     sides = (tile > 0, tile < TILE - 1, grp > 0, grp < GRP - 1)
@@ -510,20 +537,19 @@
         flag = jnp.logical_and(sides[0 if x == 0 else 1], sides[2 if y == 0 else 3])
         rim[x, y] = keep(flag, halo_c[i])
 
-    def convolve(x):
-        window = jnp.concatenate(
-            [rim[x + a, b : b + 16].reshape(256, C) for a in range(3) for b in range(3)], 1
+    def windows():
+        return jnp.concatenate(
+            [rim[pl.ds(a, 16), b : b + 16].reshape(4096, C) for a in range(3) for b in range(3)], 1
         )
-        product = dot(window, conv_flat[...])
-        rows = (
-            product[:, C : 2 * C]
-            + shift_rows(product[:, :C], True)
-            + shift_rows(product[:, 2 * C :], False)
-        )
-        pre[x] = rows
-        hidden[x] = (0.5 * rows * (1.0 + tanh_of(rows))).astype(BF16)
-
-    pl.loop(0, 16)(convolve)
+
+    product = dot(windows(), conv_flat[...])
+    rows = (
+        product[:, C : 2 * C]
+        + shift_rows(product[:, :C], True)
+        + shift_rows(product[:, 2 * C :], False)
+    )
+    pre[...] = rows.reshape(16, 256, C)
+    hidden[...] = (0.5 * rows * (1.0 + tanh_of(rows))).astype(BF16).reshape(16, 256, C)
 
     for i in range(8):
         total = hidden[2 * i].astype(F32) + hidden[2 * i + 1].astype(F32)
@@ -531,12 +557,6 @@
         feats[pl.ds(64 * i, 64), pl.ds(0, C)] = coarse
         filter1[0][:, i] = dot(z_cells[...], coarse).astype(BF16).reshape(KZ, 16, C)
 
-    def turn_windows():
-        @pl.loop(0, 18)
-        def _(x):
-            for b in range(3):
-                rim_t[x, pl.ds(C * b, C), :] = rim[x, b : b + 16].reshape(256, C).T
-
     def back_through():
         for j in range(4):
             cols = pl.ds(256 * j, 256)
@@ -553,7 +573,15 @@
         arrived(lm["grp"])
         lm["core"] = [remote(lm_all.at[core], lm_all.at[core], sem_lm3, 0, partner())]
 
-    x_filter(y_tab, x_tab, filter1, (turn_windows, gather_lm, lambda: None, swap_lm))
+    def slopes():
+        @pl.loop(0, 16)
+        def _(x):
+            value = pre[x]
+            slope = gelu_slope(value, tanh_of(value))
+            pre[x] = slope
+            base[x] = slope * (cot[x].astype(F32) * sea_of(x)).reshape(256, C)
+
+    x_filter(y_tab, x_tab, filter1, (lambda: None, gather_lm, slopes, swap_lm))
 
     arrived(lm["core"])
     for p in range(2):
@@ -610,7 +638,9 @@
             for half in range(2):
                 x = 2 * i + half
                 value = (hidden[x].astype(F32) + spread).reshape(16, 16, C)
-                out[x] = (value * sea[x].astype(F32)).astype(BF16)
+                out[x] = (value * sea_of(x)).astype(BF16)
+
+        stores[0].start()
 
     x_filter(
         y_tab,
@@ -623,33 +653,25 @@
         modes = filter2[3][:, i].reshape(128, C)
         rows = dot(z_twice[...], modes, 0, 0)[:64] + direct[pl.ds(64 * i, 64), :]
         cell_grad[i] = 0.125 * rows
-    acc[...] = jnp.zeros_like(acc)
-
-    def tap_grads(i):
+
+    first_sums.run(3)
+
+    @pl.loop(0, 8)
+    def _(i):
         spread = unpool(cell_grad[i], tmp)
-        total = None
         for half in range(2):
             x = 2 * i + half
-            upstream = (cot[x].astype(F32) * sea[x].astype(F32)).reshape(256, C) + spread
-            value = pre[x]
-            grad = (upstream * gelu_slope(value, tanh_of(value))).astype(BF16).astype(F32)
+            grad = (base[x] + spread * pre[x]).astype(BF16).astype(F32)
             shifted = jnp.concatenate(
                 [shift_rows(grad, False), grad, shift_rows(grad, True)], 1
             ).astype(BF16)
-            windows = rim_t[pl.ds(x, 3)].reshape(9 * C, 256)
-            product = dot(windows, shifted)
-            total = product if total is None else total + product
-        acc[...] += total
-
-    pl.loop(0, 4)(tap_grads)
-    first_sums.run(3)
-    pl.loop(4, 8)(tap_grads)
-
+            upstream[:, pl.ds(pl.multiple_of(256 * x, 256), 256)] = shifted.T
+
+    acc[...] = dot(upstream[...], windows()).astype(BF16)
     for c in range(3):
         for ab in range(9):
-            n = 9 * c + ab
-            rows = acc[pl.ds(C * ab, C), pl.ds(C * c, C)].astype(BF16)
-            taps_in[block_at(n)] = rows.reshape(8, 16, C)
+            rows = acc[pl.ds(C * c, C), pl.ds(C * ab, C)]
+            taps_in[block_at(9 * c + ab)] = rows.reshape(8, 16, C)
     for n in range(27, 32):
         taps_in[block_at(n)] = jnp.zeros((8, 16, C), BF16)
     last_sums.run(0)
@@ -658,6 +680,7 @@
     first_sums.run(5)
     last_sums.run(2)
     first_sums.run(6)
+    stores[1].start()
     last_sums.run(3)
 
     total = jnp.zeros((C, C), F32)
@@ -670,25 +693,75 @@
     lift_copies = spread_rows(lift_mine, lift_parts, sem_lift, "grp")
     last_sums.run(4)
     arrived(lift_copies)
+    stores[2].start()
     left(lift_copies)
+    left(halos)
     last_sums.run(5)
+    stores[3].start()
     last_sums.run(6)
-    left(halos)
-
-
-def finish_kernel(out_in, sums, taps, lift_parts, lift_own, out, conv, lift, mix, proj, sem):
-    copy = pltpu.make_async_copy(out_in, out, sem)
-    copy.start()
+    for copy in stores:
+        copy.wait()
+
+
+def finish_kernel(
+    out_in,
+    sums_in,
+    taps_in,
+    parts_in,
+    lift_in,
+    out_to,
+    conv_to,
+    lift_to,
+    mix_to,
+    proj_to,
+    out,
+    sums,
+    taps,
+    parts,
+    own_rows,
+    conv,
+    lift,
+    mix,
+    proj,
+    sems,
+):
+    def copies(first, *pairs):
+        return [
+            pltpu.make_async_copy(src, dst, sems.at[first + i])
+            for i, (src, dst) in enumerate(pairs)
+        ]
+
+    cols = pl.ds(pl.multiple_of(spot("grp") * C, C), C)
+    loads = copies(
+        0,
+        (taps_in, taps),
+        (sums_in, sums),
+        (parts_in, parts),
+        (lift_in.at[:, cols], own_rows),
+        (out_in, out),
+    )
+    stores = copies(5, (conv, conv_to), (lift, lift_to), (mix, mix_to), (proj, proj_to), (out, out_to))
+    for copy in loads:
+        copy.start()
+    loads[0].wait()
     for c in range(3):
         for ab in range(9):
-            conv[3 * ab + c] = taps[9 * c + ab].astype(F32)
+            conv[3 * ab + c] = taps[9 * c + ab].astype(F32).T
+    stores[0].start()
+    for copy in loads[1:4]:
+        copy.wait()
     for j in range(GRP):
         cols = pl.ds(C * j, C)
-        lift[:, cols] = sums[j].astype(F32) + lift_parts[j].astype(F32)
+        lift[:, cols] = sums[j].astype(F32) + parts[j].astype(F32)
         proj[j] = sums[24 + j].astype(F32)
         for p in range(2):
-            mix[p, :, cols] = dot(lift_own[...], sums[8 * (1 + p) + j], 0, 0)
-    copy.wait()
+            mix[p, :, cols] = dot(own_rows[...], sums[8 * (1 + p) + j], 0, 0)
+    for copy in stores[1:4]:
+        copy.start()
+    loads[4].wait()
+    stores[4].start()
+    for copy in stores:
+        copy.wait()
 
 
 def shards(
@@ -703,8 +776,6 @@
     kz_modes,
     cotangent,
 ):
-    sea_cells = jnp.broadcast_to(sea.astype(BF16)[..., None], field.shape)
-    vmem = pl.BlockSpec(memory_space=pltpu.VMEM)
     smem = pl.BlockSpec(memory_space=pltpu.SMEM)
     hbm = pl.BlockSpec(memory_space=pl.ANY)
     out, sums, taps, lift_parts = pl.pallas_call(
@@ -716,10 +787,11 @@
             jax.ShapeDtypeStruct((GRP, C, C), BF16),
         ),
         in_specs=[hbm] * 7 + [smem] * 3,
-        out_specs=(vmem,) * 4,
+        out_specs=(hbm,) * 4,
         scratch_shapes=[
             held(16, 16, 16, C),
-            held(16, 16, 16, C),
+            pltpu.VMEM((16, 16, 16), jnp.int32),
+            held(4096, C, dtype=F32),
             held(16, 16, 16, C),
             held(3, 3, 3, C, C),
             held(C, W),
@@ -732,11 +804,12 @@
             held(64, 64),
             held(128, 128),
             held(18, 18, 16, C),
-            held(18, 3 * C, 256),
+            held(3 * C, 4096),
             held(2, 16, 16, C),
             held(2, 16, 16, C),
             held(4, 16, C),
             held(9 * C, 3 * C),
+            held(16, 256, C, dtype=F32),
             held(16, 256, C, dtype=F32),
             held(16, 256, C),
             held(512, 3 * C),
@@ -753,11 +826,16 @@
             held(512, W),
             held(512, C, dtype=F32),
             held(8, 64, C, dtype=F32),
-            held(9 * C, 3 * C, dtype=F32),
+            held(3 * C, 9 * C),
             held(2, 2, 4, 16, 16, C),
             held(2, 2, 4, 16, 16, C),
             held(C, C),
             held(128, C, dtype=F32),
+            held(16, 16, 16, C),
+            held(2, 2, 4, 16, 16, C),
+            held(2, 2, 4, 16, 16, C),
+            held(GRP, C, C),
+            pltpu.SemaphoreType.DMA((4,)),
             pair_sems(8),
             pair_sems(GRP),
             pair_sems(GRP),
@@ -774,7 +852,7 @@
         name="step",
     )(
         field,
-        sea_cells,
+        sea,
         cotangent,
         conv_weight,
         lift_weight,
@@ -784,7 +862,6 @@
         ky_modes,
         kz_modes,
     )
-    lift_own = lax.dynamic_slice_in_dim(lift_weight, lax.axis_index("grp") * C, C, 1)
     out, conv, lift, mix, proj = pl.pallas_call(
         finish_kernel,
         out_shape=(
@@ -794,12 +871,23 @@
             jax.ShapeDtypeStruct((2, C, W), F32),
             jax.ShapeDtypeStruct((GRP, C, C), F32),
         ),
-        in_specs=[hbm] + [vmem] * 4,
-        out_specs=(hbm,) + (vmem,) * 4,
-        scratch_shapes=[pltpu.SemaphoreType.DMA(())],
-        compiler_params=pltpu.CompilerParams(vmem_limit_bytes=32 * 2**20),
+        in_specs=[hbm] * 5,
+        out_specs=(hbm,) * 5,
+        scratch_shapes=[
+            held(16, 16, 16, C),
+            held(32, C, C),
+            held(32, C, C),
+            held(GRP, C, C),
+            held(C, C),
+            held(27, C, C, dtype=F32),
+            held(C, W, dtype=F32),
+            held(2, C, W, dtype=F32),
+            held(GRP, C, C, dtype=F32),
+            pltpu.SemaphoreType.DMA((10,)),
+        ],
+        compiler_params=pltpu.CompilerParams(vmem_limit_bytes=56 * 2**20),
         name="finish",
-    )(out, sums.reshape(32, C, C), taps.reshape(32, C, C), lift_parts, lift_own)
+    )(out, sums.reshape(32, C, C), taps.reshape(32, C, C), lift_parts, lift_weight)
     return (out, conv.reshape(3, 3, 3, C, C), lift, mix, proj.reshape(W, C))
 
 

time: 128 us -> 115 us (0.90)
  local copies, waits for them, and re-layouts: 6.96 us -> 0 us
  Pallas kernels: 119 us -> 114 us
    pallas_call x1, Pallas kernels: 116 us -> 110 us  [shards(): pl.pallas_call(step_kernel, out_shape=(jax.ShapeDtypeStruct(field.shape,...]
    unnamed x8 -> x0, local copies, waits for them, and re-layouts: 4.62 us -> none
    broadcast_in_dim x1 -> x0, local copies, waits for them, and re-layouts: 1.58 us -> none  [shards(): sea_cells = jnp.broadcast_to(sea.astype(BF16)[..., None], field.shape)]
where the time goes in v2:
time: 115 us; the launch traced here: 114 us
  Pallas kernels  114 us (99%)
    pallas_call x1, Pallas kernels, shards(): pl.pallas_call(step_kernel, out_shape=(jax.ShapeDtypeStruct(field.shape,...  110 us
    pallas_call x1, Pallas kernels, shards(): pl.pallas_call(finish_kernel, out_shape=(jax.ShapeDtypeStruct(field.shape...  3.86 us

profile of v2, /device:TPU:1, one launch (start us, length us, event | category | flops | bytes accessed | tf_op | source)
XLA Modules:
  0.0 114.4 jit_solution(4398680471692007854)
XLA Ops:
  0.6 109.8 %step.1 = (bf16[16,16,16,128]{3,2,1,0:T(8,128)(2,1)}, bf16[2,2,4,16,16,128]{5,4,3,2,1,0:T(8,128)(2,1)}, bf16[2,2,4,16,16,128]{5,4,3,2,1,0:T(8,128)(2,1)}, bf16[8,128,128]{2,1,0:T(8,128)(2,1)}) custom-call(bf16[16,16,16,128]{3,2,1,0:T(8,128)(2,1)} %field_in.1, s32[16,16,16]{2,1,0:T(8,128)} %sea_in.1, bf16[16,16,16,128]{3,2,1,0:T(8,128)(2,1)} %cot_in.1, ...), custom_call_target="tpu_custom_call" | custom-call | tf_op jit(solution)/shard_map/step/pallas_call | solution.py:781
  110.4 3.9 %finish.1 = (bf16[16,16,16,128]{3,2,1,0:T(8,128)(2,1)}, f32[27,128,128]{2,1,0:T(8,128)}, f32[128,1024]{1,0:T(8,128)}, f32[2,128,1024]{2,1,0:T(8,128)}, f32[8,128,128]{2,1,0:T(8,128)}) custom-call(bf16[16,16,16,128]{3,2,1,0:T(8,128)(2,1)} %get-tuple-element.14.out_in, bf16[32,128,128]{2,1,0:T(8,128)(2,1)} %bitcast.4, bf16[32,128,128]{2,1,0:T(8,128)(2,1)} %bitcast.5, ...), custom_call_target="tpu_custom_call" | custom-call | tf_op jit(solution)/shard_map/finish/pallas_call | solution.py:865

commit v3 on v2

--- a/solution.py
+++ b/solution.py
@@ -177,63 +177,65 @@
     return lambda: pl.semaphore_wait(barrier, len(targets))
 
 
-def remote(src, dst, sems, place, device):
-    copy = pltpu.make_async_remote_copy(
+def remote(src, dst, sems, device):
+    pltpu.make_async_remote_copy(
         src_ref=src,
         dst_ref=dst,
-        send_sem=sems.at[0, place],
-        recv_sem=sems.at[1, place],
+        send_sem=sems.at[0],
+        recv_sem=sems.at[1],
         device_id=device,
         device_id_type=MESH,
-    )
-    copy.start()
-    return copy
+    ).start()
+
+
+class Sent:
+    def __init__(self, all, sems):
+        self.all, self.sems = all, sems
+
+    def wait_send(self):
+        pltpu.make_async_copy(self.all, self.all, self.sems.at[0]).wait()
+
+    def wait_recv(self):
+        pltpu.make_async_copy(self.all, self.all, self.sems.at[1]).wait()
+
+
+def to_partner(src, dst, sems):
+    remote(src, dst, sems, partner())
+    return Sent(dst, sems)
 
 
 def scatter_rows(src, slots, sems, name):
-    return [
-        (away, remote(src.at[index], slots.at[away], sems, away, device))
-        for away, index, device in group(name)
-    ]
+    for away, index, device in group(name):
+        remote(src.at[index], slots.at[away], sems, device)
+    return Sent(slots.at[pl.ds(1, size_of(name) - 1)], sems)
 
 
 def add_rows(src, slots, copies, name):
+    copies.wait_recv()
     total = src[own(name)].astype(F32)
-    for away, copy in reversed(copies):
-        copy.wait_recv()
+    for away in range(1, size_of(name)):
         total += slots[away].astype(F32)
     return total.astype(BF16)
 
 
-def exchange(src, dst, sems, name):
+def exchange(src, dst, sems, name, share=1):
     me = own(name)
-    copies = [
-        remote(src.at[index], dst.at[me], sems, away, device) for away, index, device in group(name)
-    ]
-    dst[me] = src[me]
-    return copies
+    for away, index, device in group(name):
+        remote(src.at[index // share], dst.at[me], sems, device)
+    dst[me] = src[me // share]
+    return Sent(dst.at[pl.ds(1, size_of(name) - 1)], sems)
 
 
 def spread_rows(src, dst, sems, name):
     me = own(name)
-    copies = [remote(src, dst.at[me], sems, away, device) for away, index, device in group(name)]
+    for away, index, device in group(name):
+        remote(src, dst.at[me], sems, device)
     dst[me] = src[...]
-    return copies
-
-
-def arrived(copies):
-    for copy in copies:
-        copy.wait_recv()
-
-
-def left(copies):
-    for copy in copies:
-        copy = copy[1] if isinstance(copy, tuple) else copy
-        copy.wait_send()
-
-
-def pair_sems(count):
-    return pltpu.SemaphoreType.DMA((2, count))
+    return Sent(dst.at[pl.ds(1, size_of(name) - 1)], sems)
+
+
+def pair_sems():
+    return pltpu.SemaphoreType.DMA((2,))
 
 
 def held(*shape, dtype=BF16):
@@ -245,41 +247,36 @@
     + [held(GRP, 8, 16, C) for _ in range(3)]
     + [held(TILE, 16, C) for _ in range(4)]
     + [held(256, C, dtype=F32)]
-    + [pair_sems(GRP), pair_sems(TILE), pair_sems(TILE), pair_sems(GRP)]
+    + [pair_sems() for _ in range(4)]
 )
 
 
 def x_filter(y_tab, x_tab, work, beside):
     part, got_y, sent, back, mid, got, turned, home, wide, sem1, sem2, sem3, sem4 = work
-    me = spot("grp")
-    first = [
-        remote(part.at[index // 2], got_y.at[me], sem1, away, device)
-        for away, index, device in group("grp")
-    ]
-    got_y[me] = part[me // 2]
+    first = exchange(part, got_y, sem1, "grp", 2)
     beside[0]()
-    arrived(first)
+    first.wait_recv()
     for x in range(8):
         rows = got_y[:, x].reshape(128, C)
         wide[pl.ds(x, 32, stride=8), :] = dot(y_tab[...], rows)
     mid[...] = wide[...].astype(BF16).reshape(mid.shape)
     second = exchange(mid, got, sem2, "tile")
     beside[1]()
-    arrived(second)
+    second.wait_recv()
     modes = dot(x_tab[...], got[...].reshape(TILE * 16, C)).astype(BF16)
     turned[...] = dot(x_tab[...], modes, 0, 0).astype(BF16).reshape(turned.shape)
     third = exchange(turned, home, sem3, "tile")
     beside[2]()
-    arrived(third)
+    third.wait_recv()
     wide[...] = home[...].reshape(256, C).astype(F32)
     for x in range(8):
         rows = wide[pl.ds(x, 32, stride=8), :].astype(BF16)
         sent[:, x] = dot(y_tab[...], rows, 0, 0).astype(BF16).reshape(GRP, 16, C)
     fourth = exchange(sent, back, sem4, "grp")
     beside[3]()
-    arrived(fourth)
+    fourth.wait_recv()
     for copies in (first, second, third, fourth):
-        left(copies)
+        copies.wait_send()
 
 
 SUM_SCRATCH = (
@@ -288,7 +285,7 @@
     + [held(16, 16, C) for _ in range(4)]
     + [held(16, C) for _ in range(2)]
     + [held(16, 16, C) for _ in range(2)]
-    + [pair_sems(16) for _ in range(10)]
+    + [pair_sems() for _ in range(10)]
 )
 
 
@@ -303,10 +300,9 @@
         got, mine, sa, sb, ma, mb, ra, rb, ta, tb, ga, gb = self.buffers
         core = place()["core"]
         if step == 0:
-            self.a = [remote(x.at[1 - core], got, s[0], 0, partner())]
-            self.b = []
+            self.a = to_partner(x.at[1 - core], got, s[0])
         if step == 1:
-            arrived(self.a)
+            self.a.wait_recv()
             mine[...] = (x[core].astype(F32) + got[...].astype(F32)).astype(BF16)
             self.a = scatter_rows(mine.at[0], sa, s[1], "ring_y")
             self.b = scatter_rows(mine.at[1], sb, s[2], "ring_z")
@@ -321,21 +317,20 @@
             tb[...] = add_rows(mb, rb, self.b, "xy")
             self.b = spread_rows(tb, gb, s[6], "xy")
         if step == 4:
-            arrived(self.a)
+            self.a.wait_recv()
             self.a = spread_rows(ga, y.at[core, 0], s[7], "ring_y")
-            arrived(self.b)
+            self.b.wait_recv()
             self.b = spread_rows(gb, y.at[core, 1], s[8], "ring_z")
         if step == 5:
-            arrived(self.a)
-            arrived(self.b)
-            self.a = [remote(y.at[core], self.last.at[core], s[9], 0, partner())]
-            self.b = []
+            self.a.wait_recv()
+            self.b.wait_recv()
+            self.a = to_partner(y.at[core], self.last.at[core], s[9])
         if step == 6:
-            arrived(self.a)
+            self.a.wait_recv()
             for copies in self.sent:
-                left(copies)
+                copies.wait_send()
             return
-        self.sent += [self.a, self.b]
+        self.sent += [self.a] if step in (0, 5) else [self.a, self.b]
 
 
 def block_at(n):
@@ -492,16 +487,16 @@
     met()
 
     inner = pl.ds(1, 16)
-    halos = [
-        remote(rim.at[16, inner], halo_x.at[0], sem_halo, 0, near(1, 0)),
-        remote(rim.at[1, inner], halo_x.at[1], sem_halo, 1, near(-1, 0)),
-        remote(rim.at[inner, 16], halo_y.at[0], sem_halo, 2, near(0, 1)),
-        remote(rim.at[inner, 1], halo_y.at[1], sem_halo, 3, near(0, -1)),
-        remote(rim.at[16, 16], halo_c.at[0], sem_halo, 4, near(1, 1)),
-        remote(rim.at[16, 1], halo_c.at[1], sem_halo, 5, near(1, -1)),
-        remote(rim.at[1, 16], halo_c.at[2], sem_halo, 6, near(-1, 1)),
-        remote(rim.at[1, 1], halo_c.at[3], sem_halo, 7, near(-1, -1)),
-    ]
+    strip_x, strip_y, corner = sem_halo.at[0], sem_halo.at[1], sem_halo.at[2]
+    remote(rim.at[16, 16], halo_c.at[0], corner, near(1, 1))
+    remote(rim.at[16, 1], halo_c.at[1], corner, near(1, -1))
+    remote(rim.at[1, 16], halo_c.at[2], corner, near(-1, 1))
+    remote(rim.at[1, 1], halo_c.at[3], corner, near(-1, -1))
+    remote(rim.at[16, inner], halo_x.at[0], strip_x, near(1, 0))
+    remote(rim.at[1, inner], halo_x.at[1], strip_x, near(-1, 0))
+    remote(rim.at[inner, 16], halo_y.at[0], strip_y, near(0, 1))
+    remote(rim.at[inner, 1], halo_y.at[1], strip_y, near(0, -1))
+    halos = (Sent(halo_c, corner), Sent(halo_x, strip_x), Sent(halo_y, strip_y))
     for copy in loads[2:]:
         copy.wait()
     lift_own[...] = lift[:, pl.ds(pl.multiple_of(grp * C, C), C)]
@@ -522,7 +517,8 @@
         proj_grad[pl.ds(pl.multiple_of(64 * i, 64), 64), :] = rows.astype(BF16)
 
     stacked[pl.ds(0, C), :] = lift[...]
-    arrived(halos)
+    for copies in halos:
+        copies.wait_recv()
     lm_first = scatter_rows(lm_part, lm_slots, sem_lm1, "grp")
     sides = (tile > 0, tile < TILE - 1, grp > 0, grp < GRP - 1)
 
@@ -570,8 +566,8 @@
         back_through()
 
     def swap_lm():
-        arrived(lm["grp"])
-        lm["core"] = [remote(lm_all.at[core], lm_all.at[core], sem_lm3, 0, partner())]
+        lm["grp"].wait_recv()
+        lm["core"] = to_partner(lm_all.at[core], lm_all.at[core], sem_lm3)
 
     def slopes():
         @pl.loop(0, 16)
@@ -583,12 +579,12 @@
 
     x_filter(y_tab, x_tab, filter1, (lambda: None, gather_lm, slopes, swap_lm))
 
-    arrived(lm["core"])
+    lm["core"].wait_recv()
     for p in range(2):
         for j in range(GRP):
             stacked[pl.ds(C * (p + 1), C), pl.ds(C * j, C)] = lm_all[p, j]
     for copies in (lm_first, lm["grp"], lm["core"]):
-        left(copies)
+        copies.wait_send()
 
     for i in range(8):
         modes = filter1[3][:, i].reshape(128, C)
@@ -692,10 +688,10 @@
     lift_mine[...] = total.astype(BF16)
     lift_copies = spread_rows(lift_mine, lift_parts, sem_lift, "grp")
     last_sums.run(4)
-    arrived(lift_copies)
+    lift_copies.wait_recv()
     stores[2].start()
-    left(lift_copies)
-    left(halos)
+    for copies in (lift_copies, *halos):
+        copies.wait_send()
     last_sums.run(5)
     stores[3].start()
     last_sums.run(6)
@@ -836,11 +832,11 @@
             held(2, 2, 4, 16, 16, C),
             held(GRP, C, C),
             pltpu.SemaphoreType.DMA((4,)),
-            pair_sems(8),
-            pair_sems(GRP),
-            pair_sems(GRP),
-            pair_sems(1),
-            pair_sems(GRP),
+            pltpu.SemaphoreType.DMA((3, 2)),
+            pair_sems(),
+            pair_sems(),
+            pair_sems(),
+            pair_sems(),
         ]
         + FILTER_SCRATCH()
         + FILTER_SCRATCH()

time: 115 us -> 106 us (0.922)
  Pallas kernels: 114 us -> 105 us
    pallas_call x1, Pallas kernels: 110 us -> 102 us  [shards(): pl.pallas_call(step_kernel, out_shape=(jax.ShapeDtypeStruct(field.shape,...]
where the time goes in v3:
time: 106 us
  Pallas kernels  105 us (99%)
    pallas_call x1, Pallas kernels, shards(): pl.pallas_call(step_kernel, out_shape=(jax.ShapeDtypeStruct(field.shape,...  102 us
    pallas_call x1, Pallas kernels, shards(): pl.pallas_call(finish_kernel, out_shape=(jax.ShapeDtypeStruct(field.shape...  3.86 us

profile of v3, /device:TPU:1, one launch (start us, length us, event | category | flops | bytes accessed | tf_op | source)
XLA Modules:
  0.0 106.2 jit_solution(7071959743445003517)
XLA Ops:
  0.6 101.6 %step.1 = (bf16[16,16,16,128]{3,2,1,0:T(8,128)(2,1)}, bf16[2,2,4,16,16,128]{5,4,3,2,1,0:T(8,128)(2,1)}, bf16[2,2,4,16,16,128]{5,4,3,2,1,0:T(8,128)(2,1)}, bf16[8,128,128]{2,1,0:T(8,128)(2,1)}) custom-call(bf16[16,16,16,128]{3,2,1,0:T(8,128)(2,1)} %field_in.1, s32[16,16,16]{2,1,0:T(8,128)} %sea_in.1, bf16[16,16,16,128]{3,2,1,0:T(8,128)(2,1)} %cot_in.1, ...), custom_call_target="tpu_custom_call" | custom-call | tf_op jit(solution)/shard_map/step/pallas_call | solution.py:777
  102.2 3.9 %finish.1 = (bf16[16,16,16,128]{3,2,1,0:T(8,128)(2,1)}, f32[27,128,128]{2,1,0:T(8,128)}, f32[128,1024]{1,0:T(8,128)}, f32[2,128,1024]{2,1,0:T(8,128)}, f32[8,128,128]{2,1,0:T(8,128)}) custom-call(bf16[16,16,16,128]{3,2,1,0:T(8,128)(2,1)} %get-tuple-element.14.out_in, bf16[32,128,128]{2,1,0:T(8,128)(2,1)} %bitcast.4, bf16[32,128,128]{2,1,0:T(8,128)(2,1)} %bitcast.5, ...), custom_call_target="tpu_custom_call" | custom-call | tf_op jit(solution)/shard_map/finish/pallas_call | solution.py:861

commit v4 on v3

--- a/solution.py
+++ b/solution.py
@@ -509,6 +509,38 @@
             for c in range(3):
                 conv_flat[pl.ds(C * (3 * a + b), C), pl.ds(C * c, C)] = conv_w[a, b, c]
 
+    def convolve(*boxes):
+        window = jnp.concatenate(
+            [
+                jnp.concatenate(
+                    [
+                        rim[pl.ds(x + a, nx), pl.ds(y + b, ny)].reshape(16 * nx * ny, C)
+                        for x, nx, y, ny in boxes
+                    ],
+                    0,
+                )
+                for a in range(3)
+                for b in range(3)
+            ],
+            1,
+        )
+        product = dot(window, conv_flat[...])
+        rows = (
+            product[:, C : 2 * C]
+            + shift_rows(product[:, :C], True)
+            + shift_rows(product[:, 2 * C :], False)
+        )
+        active = (0.5 * rows * (1.0 + tanh_of(rows))).astype(BF16)
+        done = 0
+        for x, nx, y, ny in boxes:
+            count = 16 * nx * ny
+            shape = (nx, ny, 16, C)
+            pre[pl.ds(x, nx), pl.ds(y, ny)] = rows[done : done + count].reshape(shape)
+            hidden[pl.ds(x, nx), pl.ds(y, ny)] = active[done : done + count].reshape(shape)
+            done += count
+
+    convolve((1, 14, 1, 14))
+
     @pl.loop(0, 8)
     def _(i):
         total = cot[2 * i].astype(F32) * sea_of(2 * i)
@@ -538,18 +570,11 @@
             [rim[pl.ds(a, 16), b : b + 16].reshape(4096, C) for a in range(3) for b in range(3)], 1
         )
 
-    product = dot(windows(), conv_flat[...])
-    rows = (
-        product[:, C : 2 * C]
-        + shift_rows(product[:, :C], True)
-        + shift_rows(product[:, 2 * C :], False)
-    )
-    pre[...] = rows.reshape(16, 256, C)
-    hidden[...] = (0.5 * rows * (1.0 + tanh_of(rows))).astype(BF16).reshape(16, 256, C)
+    convolve((0, 1, 0, 16), (15, 1, 0, 16), (1, 14, 0, 1), (1, 14, 15, 1))
 
     for i in range(8):
         total = hidden[2 * i].astype(F32) + hidden[2 * i + 1].astype(F32)
-        coarse = (0.125 * pool(total, tmp)).astype(BF16)
+        coarse = (0.125 * pool(total.reshape(256, C), tmp)).astype(BF16)
         feats[pl.ds(64 * i, 64), pl.ds(0, C)] = coarse
         filter1[0][:, i] = dot(z_cells[...], coarse).astype(BF16).reshape(KZ, 16, C)
 
@@ -572,9 +597,9 @@
     def slopes():
         @pl.loop(0, 16)
         def _(x):
-            value = pre[x]
+            value = pre[x].reshape(256, C)
             slope = gelu_slope(value, tanh_of(value))
-            pre[x] = slope
+            pre[x] = slope.reshape(16, 16, C)
             base[x] = slope * (cot[x].astype(F32) * sea_of(x)).reshape(256, C)
 
     x_filter(y_tab, x_tab, filter1, (lambda: None, gather_lm, slopes, swap_lm))
@@ -633,7 +658,7 @@
             spread = unpool(cell_grad[i], tmp)
             for half in range(2):
                 x = 2 * i + half
-                value = (hidden[x].astype(F32) + spread).reshape(16, 16, C)
+                value = hidden[x].astype(F32) + spread.reshape(16, 16, C)
                 out[x] = (value * sea_of(x)).astype(BF16)
 
         stores[0].start()
@@ -657,7 +682,7 @@
         spread = unpool(cell_grad[i], tmp)
         for half in range(2):
             x = 2 * i + half
-            grad = (base[x] + spread * pre[x]).astype(BF16).astype(F32)
+            grad = (base[x] + spread * pre[x].reshape(256, C)).astype(BF16).astype(F32)
             shifted = jnp.concatenate(
                 [shift_rows(grad, False), grad, shift_rows(grad, True)], 1
             ).astype(BF16)
@@ -805,9 +830,9 @@
             held(2, 16, 16, C),
             held(4, 16, C),
             held(9 * C, 3 * C),
+            held(16, 16, 16, C, dtype=F32),
             held(16, 256, C, dtype=F32),
-            held(16, 256, C, dtype=F32),
-            held(16, 256, C),
+            held(16, 16, 16, C),
             held(512, 3 * C),
             held(512, C),
             held(C, C),

time: 106 us -> 102 us (0.962)
  Pallas kernels: 105 us -> 102 us
    pallas_call x1, Pallas kernels: 102 us -> 97.7 us  [shards(): pl.pallas_call(step_kernel, out_shape=(jax.ShapeDtypeStruct(field.shape,...]
where the time goes in v4:
time: 102 us
  Pallas kernels  102 us (100%)
    pallas_call x1, Pallas kernels, shards(): pl.pallas_call(step_kernel, out_shape=(jax.ShapeDtypeStruct(field.shape,...  97.7 us
    pallas_call x1, Pallas kernels, shards(): pl.pallas_call(finish_kernel, out_shape=(jax.ShapeDtypeStruct(field.shape...  3.86 us

profile of v4, /device:TPU:1, one launch (start us, length us, event | category | flops | bytes accessed | tf_op | source)
XLA Modules:
  0.0 102.3 jit_solution(15674161517587108369)
XLA Ops:
  0.6 97.7 %step.1 = (bf16[16,16,16,128]{3,2,1,0:T(8,128)(2,1)}, bf16[2,2,4,16,16,128]{5,4,3,2,1,0:T(8,128)(2,1)}, bf16[2,2,4,16,16,128]{5,4,3,2,1,0:T(8,128)(2,1)}, bf16[8,128,128]{2,1,0:T(8,128)(2,1)}) custom-call(bf16[16,16,16,128]{3,2,1,0:T(8,128)(2,1)} %field_in.1, s32[16,16,16]{2,1,0:T(8,128)} %sea_in.1, bf16[16,16,16,128]{3,2,1,0:T(8,128)(2,1)} %cot_in.1, ...), custom_call_target="tpu_custom_call" | custom-call | tf_op jit(solution)/shard_map/step/pallas_call | solution.py:802
  98.3 3.9 %finish.1 = (bf16[16,16,16,128]{3,2,1,0:T(8,128)(2,1)}, f32[27,128,128]{2,1,0:T(8,128)}, f32[128,1024]{1,0:T(8,128)}, f32[2,128,1024]{2,1,0:T(8,128)}, f32[8,128,128]{2,1,0:T(8,128)}) custom-call(bf16[16,16,16,128]{3,2,1,0:T(8,128)(2,1)} %get-tuple-element.14.out_in, bf16[32,128,128]{2,1,0:T(8,128)(2,1)} %bitcast.4, bf16[32,128,128]{2,1,0:T(8,128)(2,1)} %bitcast.5, ...), custom_call_target="tpu_custom_call" | custom-call | tf_op jit(solution)/shard_map/finish/pallas_call | solution.py:886

commit v5 on v4

--- a/solution.py
+++ b/solution.py
@@ -541,14 +541,6 @@
 
     convolve((1, 14, 1, 14))
 
-    @pl.loop(0, 8)
-    def _(i):
-        total = cot[2 * i].astype(F32) * sea_of(2 * i)
-        total += cot[2 * i + 1].astype(F32) * sea_of(2 * i + 1)
-        rows = pool(total.reshape(256, C), tmp)
-        proj_grad[pl.ds(pl.multiple_of(64 * i, 64), 64), :] = rows.astype(BF16)
-
-    stacked[pl.ds(0, C), :] = lift[...]
     for copies in halos:
         copies.wait_recv()
     lm_first = scatter_rows(lm_part, lm_slots, sem_lm1, "grp")
@@ -578,6 +570,16 @@
         feats[pl.ds(64 * i, 64), pl.ds(0, C)] = coarse
         filter1[0][:, i] = dot(z_cells[...], coarse).astype(BF16).reshape(KZ, 16, C)
 
+    def outer_grads():
+        @pl.loop(0, 8)
+        def _(i):
+            total = cot[2 * i].astype(F32) * sea_of(2 * i)
+            total += cot[2 * i + 1].astype(F32) * sea_of(2 * i + 1)
+            rows = pool(total.reshape(256, C), tmp)
+            proj_grad[pl.ds(pl.multiple_of(64 * i, 64), 64), :] = rows.astype(BF16)
+
+        stacked[pl.ds(0, C), :] = lift[...]
+
     def back_through():
         for j in range(4):
             cols = pl.ds(256 * j, 256)
@@ -602,7 +604,7 @@
             pre[x] = slope.reshape(16, 16, C)
             base[x] = slope * (cot[x].astype(F32) * sea_of(x)).reshape(256, C)
 
-    x_filter(y_tab, x_tab, filter1, (lambda: None, gather_lm, slopes, swap_lm))
+    x_filter(y_tab, x_tab, filter1, (outer_grads, gather_lm, slopes, swap_lm))
 
     lm["core"].wait_recv()
     for p in range(2):

time: 102 us -> 103 us (level)
  no operation moved by 1% of the time
where the time goes in v5:
time: 103 us; the launch traced here: 102 us
  Pallas kernels  102 us (99%)
    pallas_call x1, Pallas kernels, shards(): pl.pallas_call(step_kernel, out_shape=(jax.ShapeDtypeStruct(field.shape,...  97.7 us
    pallas_call x1, Pallas kernels, shards(): pl.pallas_call(finish_kernel, out_shape=(jax.ShapeDtypeStruct(field.shape...  3.86 us

profile of v5, /device:TPU:1, one launch (start us, length us, event | category | flops | bytes accessed | tf_op | source)
XLA Modules:
  0.0 102.4 jit_solution(572640766719861759)
XLA Ops:
  0.6 97.7 %step.1 = (bf16[16,16,16,128]{3,2,1,0:T(8,128)(2,1)}, bf16[2,2,4,16,16,128]{5,4,3,2,1,0:T(8,128)(2,1)}, bf16[2,2,4,16,16,128]{5,4,3,2,1,0:T(8,128)(2,1)}, bf16[8,128,128]{2,1,0:T(8,128)(2,1)}) custom-call(bf16[16,16,16,128]{3,2,1,0:T(8,128)(2,1)} %field_in.1, s32[16,16,16]{2,1,0:T(8,128)} %sea_in.1, bf16[16,16,16,128]{3,2,1,0:T(8,128)(2,1)} %cot_in.1, ...), custom_call_target="tpu_custom_call" | custom-call | tf_op jit(solution)/shard_map/step/pallas_call | solution.py:804
  98.4 3.9 %finish.1 = (bf16[16,16,16,128]{3,2,1,0:T(8,128)(2,1)}, f32[27,128,128]{2,1,0:T(8,128)}, f32[128,1024]{1,0:T(8,128)}, f32[2,128,1024]{2,1,0:T(8,128)}, f32[8,128,128]{2,1,0:T(8,128)}) custom-call(bf16[16,16,16,128]{3,2,1,0:T(8,128)(2,1)} %get-tuple-element.14.out_in, bf16[32,128,128]{2,1,0:T(8,128)(2,1)} %bitcast.4, bf16[32,128,128]{2,1,0:T(8,128)(2,1)} %bitcast.5, ...), custom_call_target="tpu_custom_call" | custom-call | tf_op jit(solution)/shard_map/finish/pallas_call | solution.py:888
